TPU v7x, 32 devices: a whole 2x2x4 slice. The times are simulated.
32 devices in a mesh: fsdp: 4 (over y, x), ctx: 2 (over core), tp: 4 (over z).
Axes of the slice: x: 2, y: 2, z: 4, core: 2. Of those that a mesh axis runs over, the one named last changes fastest.
Arguments:
- hidden: bfloat16 [4, 4096, 1024], P('fsdp', 'ctx'), may hold values from -6 to 6
- segments: int32 [4, 4096], P('fsdp', 'ctx'), may hold values from 0 to 8, as said below
- out_grad: bfloat16 [4, 4096, 1024], P('fsdp', 'ctx'), may hold values from -6 to 6
- norm_gain: bfloat16 [1024], P(('fsdp', 'ctx')), may hold values from 0.25 to 1.75
- w_zx: bfloat16 [1024, 2, 2048], P(('fsdp', 'ctx'), None, 'tp'), may hold values from -0.1875 to 0.1875
- w_dt: bfloat16 [1024, 32], P(('fsdp', 'ctx'), 'tp'), may hold values from -0.1875 to 0.1875
- w_bc: bfloat16 [1024, 2, 128], P(('fsdp', 'ctx')), may hold values from -0.1875 to 0.1875
- conv_x_w: float32 [4, 2048], P(None, 'tp'), may hold values from -3 to 3
- conv_x_b: float32 [2048], P('tp'), may hold values from -2 to 2
- conv_bc_w: float32 [4, 2, 128], replicated, may hold values from -3 to 3
- conv_bc_b: float32 [2, 128], replicated, may hold values from -2 to 2
- dt_bias: float32 [32], P('tp'), may hold values from -5 to -2
- a_log: float32 [32], P('tp'), may hold values from -3 to 1.4
- skip_d: float32 [32], P('tp'), may hold values from 0.5 to 1.5
- out_gain: float32 [2048], P('tp'), may hold values from 0.25 to 1.75
- w_out: bfloat16 [2048, 1024], P('tp', ('fsdp', 'ctx')), may hold values from -0.125 to 0.125
Outputs:
- block_out: bfloat16 [4, 4096, 1024], P('fsdp', 'ctx')
- hidden_grad: float32 [4, 4096, 1024], P('fsdp', 'ctx')
- norm_gain_grad: float32 [1024], P(('fsdp', 'ctx'))
- w_zx_grad: float32 [1024, 2, 2048], P(('fsdp', 'ctx'), None, 'tp')
- w_dt_grad: float32 [1024, 32], P(('fsdp', 'ctx'), 'tp')
- w_bc_grad: float32 [1024, 2, 128], P(('fsdp', 'ctx'))
- conv_x_w_grad: float32 [4, 2048], P(None, 'tp')
- conv_x_b_grad: float32 [2048], P('tp')
- conv_bc_w_grad: float32 [4, 2, 128], replicated
- conv_bc_b_grad: float32 [2, 128], replicated
- dt_bias_grad: float32 [32], P('tp')
- a_log_grad: float32 [32], P('tp')
- skip_d_grad: float32 [32], P('tp')
- out_gain_grad: float32 [2048], P('tp')
- w_out_grad: float32 [2048, 1024], P('tp', ('fsdp', 'ctx'))
Inputs may be any that keep to these rules, and one draw needn't show every extreme that they name: `segments`: in every sequence the segment numbers start at 0 and rise by 0 or 1 from one token to the next; every piece of 2048 tokens holds exactly 4 document starts, none at its first or last token, so that at every boundary between pieces the tokens on both sides lie in one document.
All inputs are finite; a program needn't handle non-finite values.
Results may differ from a plain program's by a relative error of at most 0.0099.
Values may be sent and summed in bfloat16 or wider, within the bound.
No kernel may reach another device: no remote copies, remote signals or barrier semaphores. Data moves between devices by JAX's collectives and lax.ppermute only.
A program may use at most 192 MiB of HBM per device.

v0:
```python
import functools

import jax
import jax.numpy as jnp
from jax import lax
from jax.experimental import pallas as pl
from jax.experimental.pallas import tpu as pltpu
from jax.sharding import PartitionSpec as P

CHUNK = 128
STEP = 256
SUB = STEP // CHUNK
LANES = 128
EDGE = 16
GROUPS = 2
EPSILON = 1e-05
EXACT = lax.Precision.HIGHEST
F32 = jnp.float32
BF16 = jnp.bfloat16
NEGATIVE = -1e30
M1, M2, M3, ENTRY, TAIL, SEG, RAW = 16, 17, 18, 19, 20, 21, 24
VMEM_LIMIT = 56 * 1024 * 1024


def nn(a, b):
    return lax.dot_general(a, b, (((1,), (0,)), ((), ())), preferred_element_type=F32)


def nt(a, b):
    return lax.dot_general(a, b, (((1,), (1,)), ((), ())), preferred_element_type=F32)


def tn(a, b):
    return nn(a.T, b)


def exact(a, b):
    return lax.dot_general(
        a, b, (((1,), (0,)), ((), ())), precision=EXACT, preferred_element_type=F32
    )


def lasts(microseconds):
    return pl.CostEstimate(
        flops=0, bytes_accessed=int(microseconds * 3.69e6), transcendentals=0
    )


ANYWHERE = pl.BlockSpec(memory_space=pl.ANY)


def ordered(kernel, inputs, after):
    def run(*refs):
        kernel(*refs[:inputs], *refs[inputs + after :])

    return run


def iota(shape, dim):
    return lax.broadcasted_iota(jnp.int32, shape, dim)


def spread(per_head, pairs):
    rows = per_head.shape[0]
    low = iota((rows, LANES), 1) < LANES // 2
    parts = []
    for j in range(pairs):
        left = jnp.broadcast_to(per_head[:, 2 * j : 2 * j + 1], (rows, LANES))
        right = jnp.broadcast_to(per_head[:, 2 * j + 1 : 2 * j + 2], (rows, LANES))
        parts.append(jnp.where(low, left, right))
    return jnp.concatenate(parts, 1)


def halves(block):
    low = iota(block.shape, 1) < LANES // 2
    zero = jnp.zeros_like(block)
    return jnp.where(low, block, zero), jnp.where(low, zero, block)


def silu(v):
    return v * jax.nn.sigmoid(v)


def rms_unit(x):
    return x * lax.rsqrt(jnp.mean(x * x, -1, keepdims=True) + EPSILON)


def front_kernel(
    gain_lane, starts, hid, edge, tok, cw, dtp, *refs
):
    (normed, gate, pre_out, u_out, rec, st, pdx, fin, pdfin, w, gain_out,
     buf, state, decay) = refs[-14:]
    shards = refs[:-14]
    inner = gate.shape[1]
    wide = pre_out.shape[1]
    pairs = inner // LANES
    at = pl.program_id(0)

    @pl.when(at == 0)
    def _():
        for k, shard in enumerate(shards):
            size = shard.shape[0]
            w[pl.ds(pl.multiple_of(starts[k], 16), size), :] = shard[...]
        for k in range(w.shape[0] // LANES):
            tile = w[k * LANES : (k + 1) * LANES, inner + wide :].astype(F32).T
            gain_out[:, k * LANES : (k + 1) * LANES] = jnp.broadcast_to(
                tile[gain_lane : gain_lane + 1, :], (8, LANES)
            )
        edge_low = (rms_unit(edge[...].astype(F32)) * gain_out[0:1, :]).astype(BF16)
        edge_pre = nn(edge_low, w[:, inner : inner + wide])
        buf[0:8, :] = edge_pre[EDGE - 8 :, :]
        state[...] = jnp.zeros_like(state)
        decay[...] = jnp.ones_like(decay)

    @pl.when(at > 0)
    def _():
        buf[0:8, :] = buf[STEP : STEP + 8, :]

    low = (rms_unit(hid[...].astype(F32)) * gain_out[0:1, :]).astype(BF16)
    normed[...] = low
    gate[...] = nn(low, w[:, :inner])
    pre = nn(low, w[:, inner : inner + wide])
    pre_out[...] = pre
    buf[8 : 8 + STEP, :] = pre
    raw_all = nn(low, w[:, inner + wide :]) + dtp[0:1, :]
    marks = tok[...]
    u = cw[3:4, :] * pre + cw[4:5, :]
    u = u + cw[2:3, :] * (buf[7 : 7 + STEP, :] * marks[:, M1 : M1 + 1])
    u = u + cw[1:2, :] * (buf[6 : 6 + STEP, :] * marks[:, M2 : M2 + 1])
    u = u + cw[0:1, :] * (buf[5 : 5 + STEP, :] * marks[:, M3 : M3 + 1])
    u_out[...] = u
    act = silu(u)
    step_all = jax.nn.softplus(raw_all)
    lane = iota((CHUNK, LANES), 1)
    lower = (iota((CHUNK, CHUNK), 0) >= iota((CHUNK, CHUNK), 1)).astype(F32)
    for i in range(SUB):
        rows = slice(i * CHUNK, (i + 1) * CHUNK)
        step = step_all[rows]
        cum = exact(lower, step * dtp[1:2, :])
        mark = marks[rows]
        rec[rows, :] = jnp.where(
            lane < 8, cum, jnp.where(lane < 16, step, jnp.where(lane < 24, mark, raw_all[rows]))
        )
        last = cum[CHUNK - 1 :, :]
        tail = mark[:, TAIL : TAIL + 1] * jnp.exp(last - cum) * step
        fed = (act[rows, :inner] * spread(tail, pairs)).astype(BF16)
        st[i] = state[...]
        pdx[8 * i : 8 * i + 8, :] = decay[...]
        passed = spread(mark[CHUNK - 1 :, ENTRY : ENTRY + 1] * jnp.exp(last), pairs)
        input_b = act[rows, inner : inner + LANES].T.astype(BF16)
        state[...] = passed * state[...] + nn(input_b, fed)
        decay[...] = decay[...] * passed
    fin[...] = state[...]
    pdfin[...] = decay[...]


def front(hidden, edge, tok, shards, starts, gain_lane, cw, dtp, inner, wide):
    rows, width = hidden.shape
    packed = shards[0].shape[1]
    steps = rows // STEP
    state_size = LANES

    def whole(a):
        return pl.BlockSpec(a.shape, lambda i: (0,) * a.ndim)

    def tall(cols):
        return pl.BlockSpec((STEP, cols), lambda i: (i, 0))

    chunks = rows // CHUNK
    return pl.pallas_call(
        functools.partial(front_kernel, gain_lane),
        grid=(steps,),
        in_specs=[
            pl.BlockSpec(memory_space=pltpu.SMEM),
            tall(width),
            whole(edge),
            tall(LANES),
            whole(cw),
            whole(dtp),
        ]
        + [whole(shard) for shard in shards],
        out_specs=[
            tall(width),
            tall(inner),
            tall(wide),
            tall(wide),
            tall(LANES),
            pl.BlockSpec((SUB, state_size, inner), lambda i: (i, 0, 0)),
            pl.BlockSpec((8 * SUB, inner), lambda i: (i, 0)),
            pl.BlockSpec((state_size, inner), lambda i: (0, 0)),
            pl.BlockSpec((8, inner), lambda i: (0, 0)),
            pl.BlockSpec((width, packed), lambda i: (0, 0)),
            pl.BlockSpec((8, width), lambda i: (0, 0)),
        ],
        out_shape=[
            jax.ShapeDtypeStruct((rows, width), BF16),
            jax.ShapeDtypeStruct((rows, inner), F32),
            jax.ShapeDtypeStruct((rows, wide), F32),
            jax.ShapeDtypeStruct((rows, wide), F32),
            jax.ShapeDtypeStruct((rows, LANES), F32),
            jax.ShapeDtypeStruct((chunks, state_size, inner), F32),
            jax.ShapeDtypeStruct((8 * chunks, inner), F32),
            jax.ShapeDtypeStruct((state_size, inner), F32),
            jax.ShapeDtypeStruct((8, inner), F32),
            jax.ShapeDtypeStruct((width, packed), BF16),
            jax.ShapeDtypeStruct((8, width), F32),
        ],
        scratch_shapes=[
            pltpu.VMEM((STEP + 8, wide), F32),
            pltpu.VMEM((state_size, inner), F32),
            pltpu.VMEM((8, inner), F32),
        ],
        compiler_params=pltpu.CompilerParams(
            dimension_semantics=("arbitrary",), vmem_limit_bytes=VMEM_LIMIT
        ),
        cost_estimate=lasts(0.01),
        name="front",
    )(starts, hidden, edge, tok, cw, dtp, *shards)


def middle_kernel(
    u, rec, gate, st, pdx, sin, og, wo, prm,
    scan, dgate, sums, *parts,
):
    inner = gate.shape[1]
    pairs = inner // LANES
    d_gate = nn(og[...], wo[...])
    dgate[...] = d_gate
    act = silu(u[...])
    below = iota((CHUNK, CHUNK), 0) >= iota((CHUNK, CHUNK), 1)
    for i in range(SUB):
        rows = slice(i * CHUNK, (i + 1) * CHUNK)
        record = rec[rows, :]
        turned = record.T
        state = (st[i] + pdx[8 * i : 8 * i + 1, :] * sin[...]).astype(BF16)
        x = act[rows, :inner]
        input_b = act[rows, inner : inner + LANES].astype(BF16)
        input_c = act[rows, inner + LANES :].astype(BF16)
        scores = nt(input_c, input_b)
        barred = jnp.where(
            below & (record[:, SEG : SEG + 1] == turned[SEG : SEG + 1, :]), 0.0, NEGATIVE
        )
        entry = record[:, ENTRY : ENTRY + 1] * jnp.exp(record)
        outs = []
        for j in range(pairs):
            block = x[:, j * LANES : (j + 1) * LANES].astype(BF16)
            total = None
            for k, side in enumerate(halves(block)):
                h = 2 * j + k
                link = jnp.exp(record[:, h : h + 1] - turned[h : h + 1, :] + barred)
                weight = (scores * link * turned[8 + h : 9 + h, :]).astype(BF16)
                term = nn(weight, side)
                total = term if total is None else total + term
            outs.append(total)
        y = jnp.concatenate(outs, 1)
        y = y + nn(input_c, state) * spread(entry, pairs) + prm[0:1, :] * x
        scan[rows, :] = y
    gated = scan[...] * silu(gate[...])
    scaled = gated * prm[1:2, :]
    squares = jnp.sum(gated * gated, -1, keepdims=True)
    crosses = jnp.sum(scaled * d_gate, -1, keepdims=True)
    lane = iota((STEP, LANES), 1)
    both = jnp.where(lane == 0, squares, jnp.where(lane == 1, crosses, 0.0))
    sums[...] = both.T[0:8, :]
    part_low = nt(scaled.astype(BF16), wo[...]).astype(BF16)
    steps_each = pl.num_programs(0) // len(parts)
    for k, part in enumerate(parts):

        @pl.when(pl.program_id(0) // steps_each == k)
        def _():
            part[...] = part_low


def middle(u, rec, gate, st, pdx, sin, og, wo, prm):
    rows, inner = gate.shape
    width = og.shape[1]
    steps = rows // STEP
    each = steps // GROUPS

    def whole(a):
        return pl.BlockSpec(a.shape, lambda i: (0,) * a.ndim)

    def tall(cols):
        return pl.BlockSpec((STEP, cols), lambda i: (i, 0))

    def part(k):
        return pl.BlockSpec((STEP, width), lambda i: (jnp.clip(i - k * each, 0, each - 1), 0))

    return pl.pallas_call(
        middle_kernel,
        grid=(steps,),
        in_specs=[
            tall(u.shape[1]),
            tall(LANES),
            tall(inner),
            pl.BlockSpec((SUB,) + st.shape[1:], lambda i: (i, 0, 0)),
            pl.BlockSpec((8 * SUB, inner), lambda i: (i, 0)),
            whole(sin),
            tall(width),
            whole(wo),
            whole(prm),
        ],
        out_specs=[
            tall(inner),
            tall(inner),
            pl.BlockSpec((8, STEP), lambda i: (0, i)),
        ]
        + [part(k) for k in range(GROUPS)],
        out_shape=[
            jax.ShapeDtypeStruct((rows, inner), F32),
            jax.ShapeDtypeStruct((rows, inner), F32),
            jax.ShapeDtypeStruct((8, rows), F32),
        ]
        + [jax.ShapeDtypeStruct((rows // GROUPS, width), BF16)] * GROUPS,
        compiler_params=pltpu.CompilerParams(
            dimension_semantics=("arbitrary",), vmem_limit_bytes=VMEM_LIMIT
        ),
        cost_estimate=lasts(0.01),
        name="middle",
    )(u, rec, gate, st, pdx, sin, og, wo, prm)


def turn_kernel(
    inner_total, scan, gate, dgate, sums, upre_c, rec, prm,
    dscan, dgr, glow, adj, psx, fin, gain_grad,
    state, decay,
):
    inner = gate.shape[1]
    pairs = inner // LANES
    at = pl.program_id(0)

    @pl.when(at == 0)
    def _():
        state[...] = jnp.zeros_like(state)
        decay[...] = jnp.ones_like(decay)
        gain_grad[...] = jnp.zeros_like(gain_grad)

    head = sums[...]
    column = jnp.concatenate([head, jnp.zeros((LANES - 8, STEP), F32)], 0).T
    inv = lax.rsqrt(column[:, 0:1] / inner_total + EPSILON)
    cube = inv * inv * inv * (column[:, 1:2] / inner_total)
    raw = gate[...]
    sig = jax.nn.sigmoid(raw)
    sil = raw * sig
    y = scan[...]
    gated = y * sil
    unit = gated * inv
    d_gate = dgate[...]
    gain = prm[1:2, :]
    glow[...] = (unit * gain).astype(BF16)
    gain_grad[...] += jnp.broadcast_to(jnp.sum(d_gate * unit, 0, keepdims=True), gain_grad.shape)
    d_gated = inv * gain * d_gate - gated * cube
    d_scan = d_gated * sil
    dscan[...] = d_scan
    dgr[...] = (d_gated * y * (sig * (1.0 + raw * (1.0 - sig)))).astype(BF16)
    input_c = silu(upre_c[...])
    for i in reversed(range(SUB)):
        rows = slice(i * CHUNK, (i + 1) * CHUNK)
        record = rec[rows, :]
        entry = record[:, ENTRY : ENTRY + 1] * jnp.exp(record)
        adj[i] = state[...]
        psx[8 * i : 8 * i + 8, :] = decay[...]
        passed = spread(entry[CHUNK - 1 :, :], pairs)
        fed = (d_scan[rows] * spread(entry, pairs)).astype(BF16)
        state[...] = passed * state[...] + nn(input_c[rows].T.astype(BF16), fed)
        decay[...] = decay[...] * passed
    fin[...] = state[...]


def turn(scan, gate, dgate, sums, u, rec, prm, inner_total):
    rows, inner = scan.shape
    steps = rows // STEP
    chunks = rows // CHUNK
    state_size = LANES
    c_block = u.shape[1] // LANES - 1

    def whole(a):
        return pl.BlockSpec(a.shape, lambda i: (0,) * a.ndim)

    def tall(cols):
        return pl.BlockSpec((STEP, cols), lambda i: (steps - 1 - i, 0))

    return pl.pallas_call(
        functools.partial(turn_kernel, float(inner_total)),
        grid=(steps,),
        in_specs=[
            tall(inner),
            tall(inner),
            tall(inner),
            pl.BlockSpec((8, STEP), lambda i: (0, steps - 1 - i)),
            pl.BlockSpec((STEP, LANES), lambda i: (steps - 1 - i, c_block)),
            tall(LANES),
            whole(prm),
        ],
        out_specs=[
            tall(inner),
            tall(inner),
            tall(inner),
            pl.BlockSpec((SUB, state_size, inner), lambda i: (steps - 1 - i, 0, 0)),
            pl.BlockSpec((8 * SUB, inner), lambda i: (steps - 1 - i, 0)),
            pl.BlockSpec((state_size, inner), lambda i: (0, 0)),
            pl.BlockSpec((8, inner), lambda i: (0, 0)),
        ],
        out_shape=[
            jax.ShapeDtypeStruct((rows, inner), F32),
            jax.ShapeDtypeStruct((rows, inner), BF16),
            jax.ShapeDtypeStruct((rows, inner), BF16),
            jax.ShapeDtypeStruct((chunks, state_size, inner), F32),
            jax.ShapeDtypeStruct((8 * chunks, inner), F32),
            jax.ShapeDtypeStruct((state_size, inner), F32),
            jax.ShapeDtypeStruct((8, inner), F32),
        ],
        scratch_shapes=[pltpu.VMEM((state_size, inner), F32), pltpu.VMEM((8, inner), F32)],
        compiler_params=pltpu.CompilerParams(
            dimension_semantics=("arbitrary",), vmem_limit_bytes=VMEM_LIMIT
        ),
        cost_estimate=lasts(0.01),
        name="turn",
    )(scan, gate, dgate, sums, u, rec, prm)


def back_kernel(
    u, rec, dscan, st, pdx, sin, adj, psx, ain, prm, dtp,
    dpre, dstep, skip_acc, head_acc,
):
    inner = dscan.shape[1]
    pairs = inner // LANES
    heads = 2 * pairs

    @pl.when(pl.program_id(0) == 0)
    def _():
        skip_acc[...] = jnp.zeros_like(skip_acc)
        head_acc[...] = jnp.zeros_like(head_acc)

    raw = u[...]
    sig = jax.nn.sigmoid(raw)
    act = raw * sig
    slope = sig * (1.0 + raw * (1.0 - sig))
    above = iota((CHUNK, CHUNK), 0) <= iota((CHUNK, CHUNK), 1)
    upper = above.astype(F32)
    lane = iota((CHUNK, LANES), 1)
    gather_heads = (iota((inner, LANES), 0) // (LANES // 2) == iota((inner, LANES), 1)).astype(BF16)
    nega = dtp[1:2, :]
    for i in range(SUB):
        rows = slice(i * CHUNK, (i + 1) * CHUNK)
        record = rec[rows, :]
        turned = record.T
        state = st[i] + pdx[8 * i : 8 * i + 1, :] * sin[...]
        state_low = state.astype(BF16)
        later = adj[i] + psx[8 * i : 8 * i + 1, :] * ain[...]
        later_low = later.astype(BF16)
        x = act[rows, :inner]
        b_wide = act[rows, inner : inner + LANES]
        c_wide = act[rows, inner + LANES :]
        input_b = b_wide.astype(BF16)
        input_c = c_wide.astype(BF16)
        dy = dscan[rows, :]
        scores = nt(input_b, input_c)
        barred = jnp.where(
            above & (record[:, SEG : SEG + 1] == turned[SEG : SEG + 1, :]), 0.0, NEGATIVE
        )
        step = pltpu.roll(record, LANES - 8, axis=1)
        z = pltpu.roll(record, LANES - RAW, axis=1)
        d_scores = jnp.zeros((CHUNK, CHUNK), F32)
        direct = jnp.zeros((CHUNK, LANES), F32)
        arrivals = []
        dxs = []
        for j in range(pairs):
            cols = slice(j * LANES, (j + 1) * LANES)
            x_sides = halves(x[:, cols].astype(BF16))
            dy_pair = dy[:, cols].astype(BF16)
            dy_sides = halves(dy_pair)
            total = None
            for k in range(2):
                h = 2 * j + k
                step_col = record[:, 8 + h : 9 + h]
                link = jnp.exp(turned[h : h + 1, :] - record[:, h : h + 1] + barred)
                d_link = nt(x_sides[k], dy_pair) * link
                d_scaled = d_link * step_col
                d_scores = d_scores + d_scaled
                flow = d_scaled * scores
                arrivals.append(jnp.sum(flow, 0, keepdims=True))
                given = jnp.sum(d_link * scores, 1, keepdims=True)
                direct = jnp.where(lane == h, given, direct)
                weight = (scores * link * step_col).astype(BF16)
                term = nn(weight, dy_sides[k])
                total = term if total is None else total + term
            dxs.append(total)
        dx = jnp.concatenate(dxs, 1)
        arrived = jnp.concatenate(arrivals + [jnp.zeros((CHUNK - heads, CHUNK), F32)], 0).T
        decay_in = record[:, ENTRY : ENTRY + 1] * jnp.exp(record)
        last = record[CHUNK - 1 :, :]
        tail_exp = record[:, TAIL : TAIL + 1] * jnp.exp(last - record)
        tail = tail_exp * step
        tail_wide = spread(jnp.where(lane < 8, tail, 0.0), pairs)
        fed_back = (dy * spread(decay_in, pairs)).astype(BF16)
        fed = (x * tail_wide).astype(BF16)
        from_state = nn(input_c, state_low)
        d_fed = nn(input_b, later_low)
        d_score_low = d_scores.astype(BF16)
        d_c = nt(fed_back, state_low) + nn(d_scores.T.astype(BF16), input_b)
        d_b = nt(fed, later_low) + nn(d_score_low, input_c)
        d_entry = nn((dy * from_state).astype(BF16), gather_heads)
        d_tail = nn((x * d_fed).astype(BF16), gather_heads)
        through = jnp.broadcast_to(jnp.sum(later * state, 0, keepdims=True), (16, inner))
        d_through = nn(through.astype(BF16), gather_heads)[0:1, :]
        dx = dx + d_fed * tail_wide + prm[0:1, :] * dy
        tail_flow = d_tail * tail
        d_cum = arrived - direct * step + d_entry * decay_in - tail_flow
        d_cum = jnp.where(lane < 8, d_cum, 0.0)
        d_last = jnp.sum(tail_flow, 0, keepdims=True) + decay_in[CHUNK - 1 :, :] * d_through
        d_rate = exact(upper, d_cum) + jnp.where(lane < 8, d_last, 0.0)
        d_step = direct + d_tail * tail_exp + nega * d_rate
        d_z = jnp.where(lane < 8, d_step * jax.nn.sigmoid(z), 0.0)
        dstep[rows, :] = d_z.astype(BF16)
        dpre[rows, :] = jnp.concatenate([dx, d_b, d_c], 1) * slope[rows]
        skip_acc[...] += jnp.broadcast_to(jnp.sum(dy * x, 0, keepdims=True), skip_acc.shape)
        head_acc[0:1, :] += jnp.sum(d_z, 0, keepdims=True)
        head_acc[1:2, :] += jnp.sum(
            jnp.where(lane < 8, d_rate * (nega * step), 0.0), 0, keepdims=True
        )


def back(u, rec, dscan, st, pdx, sin, adj, psx, ain, prm, dtp, after, group):
    rows, wide = u.shape
    inner = dscan.shape[1]
    steps = rows // STEP // GROUPS
    first = group * steps

    def whole(a):
        return pl.BlockSpec(a.shape, lambda i: (0,) * a.ndim)

    def tall(cols):
        return pl.BlockSpec((STEP, cols), lambda i: (first + i, 0))

    def out_tall(cols):
        return pl.BlockSpec((STEP, cols), lambda i: (i, 0))

    def states(at):
        return pl.BlockSpec((SUB,) + st.shape[1:], lambda i: (at + i, 0, 0))

    def decays(at):
        return pl.BlockSpec((8 * SUB, inner), lambda i: (at + i, 0))

    return pl.pallas_call(
        ordered(back_kernel, 11, len(after)),
        grid=(steps,),
        in_specs=[
            tall(wide),
            tall(LANES),
            tall(inner),
            states(first),
            decays(first),
            whole(sin),
            states(first),
            decays(first),
            whole(ain),
            whole(prm),
            whole(dtp),
        ]
        + [ANYWHERE] * len(after),
        out_specs=[
            out_tall(wide),
            out_tall(LANES),
            pl.BlockSpec((8, inner), lambda i: (0, 0)),
            pl.BlockSpec((8, LANES), lambda i: (0, 0)),
        ],
        out_shape=[
            jax.ShapeDtypeStruct((steps * STEP, wide), F32),
            jax.ShapeDtypeStruct((steps * STEP, LANES), BF16),
            jax.ShapeDtypeStruct((8, inner), F32),
            jax.ShapeDtypeStruct((8, LANES), F32),
        ],
        compiler_params=pltpu.CompilerParams(
            dimension_semantics=("arbitrary",), vmem_limit_bytes=VMEM_LIMIT
        ),
        cost_estimate=lasts(0.01),
        name="back",
    )(u, rec, dscan, st, pdx, sin, adj, psx, ain, prm, dtp, *after)


def rear_kernel(
    dpre, rec, pre, dgr, dstep, follow, w, cw,
    dproj, dnorm, conv_acc,
    buf, mbuf,
):
    wide = dpre.shape[1]
    inner = dgr.shape[1]

    @pl.when(pl.program_id(0) == 0)
    def _():
        buf[STEP : STEP + 8, :] = follow[:, :wide]
        mbuf[STEP : STEP + 8, :] = follow[:, wide:]
        conv_acc[...] = jnp.zeros_like(conv_acc)

    @pl.when(pl.program_id(0) > 0)
    def _():
        buf[STEP : STEP + 8, :] = buf[0:8, :]
        mbuf[STEP : STEP + 8, :] = mbuf[0:8, :]

    grad = dpre[...]
    buf[0:STEP, :] = grad
    mbuf[0:STEP, :] = rec[...]
    value = pre[...]
    total = cw[3:4, :] * grad
    conv_acc[3:4, :] += jnp.sum(value * grad, 0, keepdims=True)
    conv_acc[4:5, :] += jnp.sum(grad, 0, keepdims=True)
    for shift in (1, 2, 3):
        mark = mbuf[shift : shift + STEP, :][:, M1 + shift - 1 : M1 + shift]
        moved = buf[shift : shift + STEP, :] * mark
        total = total + cw[3 - shift : 4 - shift, :] * moved
        conv_acc[3 - shift : 4 - shift, :] += jnp.sum(value * moved, 0, keepdims=True)
    dproj[:, :inner] = dgr[...]
    dproj[:, inner : inner + wide] = total.astype(BF16)
    dproj[:, inner + wide :] = dstep[...]
    dnorm[...] = nt(dproj[...], w[...]).astype(BF16)


def rear(dpre, rec, pre, dgr, dstep, follow, w, cw, after, group):
    rows, wide = dpre.shape
    steps = rows // STEP
    inner = dgr.shape[1]
    width, packed = w.shape
    first = group * steps

    def whole(a):
        return pl.BlockSpec(a.shape, lambda i: (0,) * a.ndim)

    def tall(cols):
        return pl.BlockSpec((STEP, cols), lambda i: (first + steps - 1 - i, 0))

    def own(cols):
        return pl.BlockSpec((STEP, cols), lambda i: (steps - 1 - i, 0))

    return pl.pallas_call(
        ordered(rear_kernel, 8, len(after)),
        grid=(steps,),
        in_specs=[
            own(wide),
            tall(LANES),
            tall(wide),
            tall(inner),
            own(LANES),
            whole(follow),
            whole(w),
            whole(cw),
        ]
        + [ANYWHERE] * len(after),
        out_specs=[
            own(packed),
            own(width),
            pl.BlockSpec((8, wide), lambda i: (0, 0)),
        ],
        out_shape=[
            jax.ShapeDtypeStruct((rows, packed), BF16),
            jax.ShapeDtypeStruct((rows, width), BF16),
            jax.ShapeDtypeStruct((8, wide), F32),
        ],
        scratch_shapes=[
            pltpu.VMEM((STEP + 8, wide), F32),
            pltpu.VMEM((STEP + 8, LANES), F32),
        ],
        compiler_params=pltpu.CompilerParams(
            dimension_semantics=("arbitrary",), vmem_limit_bytes=VMEM_LIMIT
        ),
        cost_estimate=lasts(0.01),
        name="rear",
    )(dpre, rec, pre, dgr, dstep, follow, w, cw, *after)


def settle_kernel(inner_total, hid, sums, given, held, outer, filled, out):
    column = jnp.concatenate([sums[...], jnp.zeros((LANES - 8, STEP), F32)], 0).T
    inv = lax.rsqrt(column[:, 0:1] / inner_total + EPSILON)
    total = jnp.where(outer[0:1, 0:1] > 0.0, given[...].astype(F32), held[...].astype(F32))
    out[...] = (hid[...].astype(F32) + inv * total).astype(BF16)


def finish_kernel(hid, cot, gain, given, held, outer, filled, out):
    x = hid[...].astype(F32)
    inv = lax.rsqrt(jnp.mean(x * x, -1, keepdims=True) + EPSILON)
    total = jnp.where(outer[0:1, 0:1] > 0.0, given[...].astype(F32), held[...].astype(F32))
    scaled = total * gain[0:1, :]
    cross = jnp.mean(scaled * x, -1, keepdims=True)
    out[...] = cot[...].astype(F32) + inv * scaled - x * (inv * inv * inv * cross)


def by_group(kernel, out_like, dtype, group, fresh, operands, filled, after, name):
    rows, width = out_like.shape
    steps = rows // GROUPS // STEP
    first = group * steps
    specs = {
        "all": lambda a: pl.BlockSpec((STEP, a.shape[1]), lambda i: (first + i, 0)),
        "group": lambda a: pl.BlockSpec((STEP, a.shape[1]), lambda i: (i, 0)),
        "columns": lambda a: pl.BlockSpec((8, STEP), lambda i: (0, first + i)),
        "whole": lambda a: pl.BlockSpec(a.shape, lambda i: (0, 0)),
    }
    count = len(operands) + 1
    return pl.pallas_call(
        ordered(kernel, count, len(after)),
        grid=(steps,),
        in_specs=[specs[kind](a) for a, kind in operands] + [ANYWHERE] * (1 + len(after)),
        out_specs=pl.BlockSpec((STEP, width), lambda i: (first + i, 0)),
        out_shape=jax.ShapeDtypeStruct((rows, width), dtype),
        input_output_aliases={} if fresh else {count - 1: 0},
        compiler_params=pltpu.CompilerParams(
            dimension_semantics=("arbitrary",), vmem_limit_bytes=VMEM_LIMIT
        ),
        cost_estimate=lasts(0.01),
        name=name,
    )(*[a for a, _ in operands], filled, *after)


def passed_along(value, axis, steps):
    count = lax.axis_size(axis)
    leading, last = (max(0, -steps), min(count, count - steps))
    return lax.ppermute(value, axis, [(source, source + steps) for source in range(leading, last)])


def chained(own, decay, axis, steps):
    entering = jnp.zeros_like(own)
    for turn_at in range(lax.axis_size(axis) - 1):
        leaving = own if turn_at == 0 else own + decay * entering
        entering = passed_along(leaving, axis, steps)
    return entering


def butterfly_sum(value, axis):
    bit = 1
    while bit < lax.axis_size(axis):
        pairs = [(i, i ^ bit) for i in range(lax.axis_size(axis))]
        value = value + lax.ppermute(value, axis, pairs)
        bit *= 2
    return value


def join_kernel(pairs, *refs):
    outs = refs[2 * pairs :]
    for k in range(pairs):
        left, right, out = refs[2 * k], refs[2 * k + 1], outs[k]
        out[...] = (left[...].astype(F32) + right[...].astype(F32)).astype(out.dtype)


def join(pairs, after, held=()):
    rows, width = pairs[0][0].shape
    spec = pl.BlockSpec((STEP, width), lambda i: (i, 0))
    return pl.pallas_call(
        ordered(
            functools.partial(join_kernel, len(pairs)), 2 * len(pairs), len(after) + len(held)
        ),
        grid=(rows // STEP,),
        in_specs=[spec] * (2 * len(pairs)) + [ANYWHERE] * (len(after) + len(held)),
        out_specs=[spec] * len(pairs) + [ANYWHERE] * len(held),
        out_shape=[jax.ShapeDtypeStruct((rows, width), BF16)] * len(pairs)
        + [jax.ShapeDtypeStruct(a.shape, a.dtype) for a in held],
        input_output_aliases={
            2 * len(pairs) + len(after) + k: len(pairs) + k for k in range(len(held))
        },
        compiler_params=pltpu.CompilerParams(
            dimension_semantics=("arbitrary",), vmem_limit_bytes=VMEM_LIMIT
        ),
        cost_estimate=lasts(0.01),
        name="join",
    )(*[a for pair in pairs for a in pair], *after, *held)


class LineSum:
    def __init__(self, value):
        self.own = value
        self.come = lax.ppermute(value, "tp", [(0, 1), (3, 2)])
        self.near = self.across = self.given = None

    def pair(self):
        return (self.own if self.near is None else self.near, self.come)

    def joined(self, value):
        if self.near is None:
            self.near = value
            self.come = lax.ppermute(value, "tp", [(1, 2), (2, 1)])
        else:
            self.across = value
            self.given = lax.ppermute(value, "tp", [(1, 0), (2, 3)])


def advance(sums, after, held=()):
    outs = join([one.pair() for one in sums], after, held)
    for one, value in zip(sums, outs):
        one.joined(value)
    return tuple(outs)


def total_kernel(own, one, two, three, *refs):
    out = refs[len(refs) // 2]
    out[...] = (own[...] + one[...]) + (two[...] + three[...])


def total_over_row(own, held):
    others = [lax.ppermute(own, "tp", [(i, i ^ bits) for i in range(4)]) for bits in (1, 2, 3)]
    spec = pl.BlockSpec(own.shape, lambda i: (0, 0))
    return pl.pallas_call(
        total_kernel,
        grid=(1,),
        in_specs=[spec] * 4 + [ANYWHERE] * len(held),
        out_specs=[spec] + [ANYWHERE] * len(held),
        out_shape=[jax.ShapeDtypeStruct(own.shape, own.dtype)]
        + [jax.ShapeDtypeStruct(a.shape, a.dtype) for a in held],
        input_output_aliases={4 + k: 1 + k for k in range(len(held))},
        cost_estimate=lasts(0.01),
        name="total",
    )(own, *others, *held)


def other_core_kernel(place, w, wo, out):
    packed = w.shape[1]
    out[:, :packed] = w[...].astype(BF16)
    out[:, packed:] = wo[...].astype(BF16)


def split_kernel(
    place, w_ka, w_sa, w_kb, w_sb, wo_kb, wo_sb, r_ka, r_sa, r_kb, r_sb,
    keep_a, send_a, keep_b, send_b,
):
    cut, packed = keep_a.shape[1], w_ka.shape[1]
    keep_a[...] = w_ka[:, :cut] + r_ka[:, :cut].astype(F32)
    send_a[...] = (w_sa[:, :cut] + r_sa[:, :cut].astype(F32)).astype(BF16)
    for w, wo, r, out in ((w_kb, wo_kb, r_kb, keep_b), (w_sb, wo_sb, r_sb, send_b)):
        out[:, : packed - cut] = (w[:, cut:] + r[:, cut:packed].astype(F32)).astype(out.dtype)
        out[:, packed - cut :] = (wo[...] + r[:, packed:].astype(F32)).astype(out.dtype)


def second_kernel(place, ka, ra, sa, rsa, kb, rb, sb, rsb, keep_a, send_a, keep_b, send_b):
    keep_a[...] = ka[...] + ra[...].astype(F32)
    send_a[...] = (sa[...] + rsa[...].astype(F32)).astype(BF16)
    keep_b[...] = kb[...] + rb[...].astype(F32)
    send_b[...] = (sb[...] + rsb[...].astype(F32)).astype(BF16)


def placed_call(kernel, steps, place, inputs, outputs, name, after=()):
    return pl.pallas_call(
        ordered(kernel, 1 + len(inputs), len(after)),
        grid_spec=pltpu.PrefetchScalarGridSpec(
            num_scalar_prefetch=1,
            grid=(steps,),
            in_specs=[
                pl.BlockSpec((LANES, a.shape[1]), functools.partial(lambda f, i, p: (f(i, p), 0), f))
                for a, f in inputs
            ]
            + [ANYWHERE] * len(after),
            out_specs=[pl.BlockSpec((LANES, cols), lambda i, p: (i, 0)) for cols, _ in outputs],
        ),
        out_shape=[jax.ShapeDtypeStruct((steps * LANES, cols), kind) for cols, kind in outputs],
        compiler_params=pltpu.CompilerParams(
            dimension_semantics=("arbitrary",), vmem_limit_bytes=VMEM_LIMIT
        ),
        cost_estimate=lasts(0.01),
        name=name,
    )(place, *[a for a, _ in inputs], *after)


def to_owners(w, wo):
    after = yield
    packed, extra = w.shape[1], wo.shape[1]
    if lax.axis_size("fsdp") != 4 or lax.axis_size("ctx") != 2 or w.shape[0] != 8 * LANES:
        both = jnp.concatenate([w, wo], 1)
        summed = lax.psum_scatter(both, ("fsdp", "ctx"), scatter_dimension=0, tiled=True)
        yield w
        yield w
        yield w
        yield summed
        return

    def swapped(value, axis, bit):
        count = lax.axis_size(axis)
        return lax.ppermute(value, axis, [(i, i ^ bit) for i in range(count)])

    fsdp = lax.axis_index("fsdp")
    place = jnp.stack([fsdp % 2, fsdp // 2, lax.axis_index("ctx")]).astype(jnp.int32)
    cut = 1024
    rest = packed + extra - cut

    (sent,) = placed_call(
        other_core_kernel, 4, place,
        [(w, lambda i, p: 2 * i + 1 - p[2]), (wo, lambda i, p: 2 * i + 1 - p[2])],
        [(packed + extra, BF16)], "other_core", after,
    )
    come = swapped(sent, "ctx", 1)
    after = yield sent
    of = {
        "ka": lambda i, p: 2 * i + p[0],
        "sa": lambda i, p: 2 * i + 1 - p[0],
        "kb": lambda i, p: 2 * p[1] + i,
        "sb": lambda i, p: 2 * (1 - p[1]) + i,
    }

    def own(key):
        return lambda i, p: 2 * of[key](i, p) + p[2]

    keep_a, send_a, keep_b, send_b = placed_call(
        split_kernel, 2, place,
        [(w, own(key)) for key in ("ka", "sa", "kb", "sb")]
        + [(wo, own(key)) for key in ("kb", "sb")]
        + [(come, of[key]) for key in ("ka", "sa", "kb", "sb")],
        [(cut, F32), (cut, BF16), (rest, F32), (rest, BF16)], "split", after,
    )
    come_a, come_b = swapped(send_a, "fsdp", 1), swapped(send_b, "fsdp", 2)
    after = yield send_a
    y, not_y = (lambda i, p: p[1]), (lambda i, p: 1 - p[1])
    x, not_x = (lambda i, p: p[0]), (lambda i, p: 1 - p[0])
    keep_a, send_a, keep_b, send_b = placed_call(
        second_kernel, 1, place,
        [(keep_a, y), (come_a, y), (keep_a, not_y), (come_a, not_y)]
        + [(keep_b, x), (come_b, x), (keep_b, not_x), (come_b, not_x)],
        [(cut, F32), (cut, BF16), (rest, F32), (rest, BF16)], "second", after,
    )
    come_a, come_b = swapped(send_a, "fsdp", 2), swapped(send_b, "fsdp", 1)
    yield send_a
    yield jnp.concatenate([keep_a + come_a.astype(F32), keep_b + come_b.astype(F32)], 1)


def flip_kernel(value, out):
    out[...] = value[...].astype(F32).T.astype(out.dtype)


def flipped(value, after):
    rows, cols = value.shape
    return pl.pallas_call(
        ordered(flip_kernel, 1, len(after)),
        grid=(1,),
        in_specs=[pl.BlockSpec((rows, cols), lambda i: (0, 0))] + [ANYWHERE] * len(after),
        out_specs=pl.BlockSpec((cols, rows), lambda i: (0, 0)),
        out_shape=jax.ShapeDtypeStruct((cols, rows), value.dtype),
        cost_estimate=lasts(0.01),
        name="flip",
    )(value, *after)


def gathered_shards(own):
    rows = own.shape[0]
    if lax.axis_size("fsdp") != 4 or lax.axis_size("ctx") != 2:
        return [lax.all_gather(own, ("fsdp", "ctx"), axis=0, tiled=True)], [0]

    def swapped(value, axis, bit):
        count = lax.axis_size(axis)
        return lax.ppermute(value, axis, [(i, i ^ bit) for i in range(count)])

    half = rows // 2
    by_one, by_two = swapped(own, "fsdp", 1), swapped(own, "fsdp", 2)
    upper = swapped(by_two[:half], "fsdp", 1)
    under = swapped(by_one[half:], "fsdp", 2)
    mine = [own, by_one, by_two, upper, under]
    place = lax.axis_index("fsdp")
    core = lax.axis_index("ctx")
    shards, starts = [], []
    for other in (0, 1):
        for value, bits, offset in zip(mine, (0, 1, 2, 3, 3), (0, 0, 0, 0, half)):
            shards.append(swapped(value, "ctx", 1) if other else value)
            starts.append(((place ^ bits) * 2 + (core ^ other)) * rows + offset)
    return shards, starts


def token_marks(segment, before):
    rows = segment.shape[0]
    joined = jnp.concatenate([before, segment])
    marks = [joined[3 - j : 3 - j + rows] == segment for j in (1, 2, 3)]
    blocks = segment.reshape(-1, CHUNK)
    previous = jnp.concatenate([before[2:], blocks[:-1, -1]])
    marks.append((blocks == previous[:, None]).reshape(-1))
    marks.append((blocks == blocks[:, -1:]).reshape(-1))
    marks.append(segment)
    table = jnp.stack([mark.astype(F32) for mark in marks], 1)
    return jnp.pad(table, ((0, 0), (M1, LANES - M1 - len(marks))))


def body(
    hidden, segments, out_grad, norm_gain, w_zx, w_dt, w_bc, conv_x_w, conv_x_b,
    conv_bc_w, conv_bc_b, dt_bias, a_log, skip_d, out_gain, w_out,
):
    _, rows, width = hidden.shape
    inner = w_zx.shape[2]
    heads = w_dt.shape[1]
    head_size = inner // heads
    state_size = w_bc.shape[2]
    wide = inner + 2 * state_size
    taps = conv_x_w.shape[0]
    owned = w_zx.shape[0]
    shards = ("fsdp", "ctx")
    hid = hidden[0]
    cot = out_grad[0]
    segment = segments[0]

    packed = jnp.concatenate(
        [
            w_zx.reshape(owned, 2 * inner),
            w_bc.reshape(owned, 2 * state_size),
            w_dt, w_dt, w_dt, w_dt,
            norm_gain[:, None],
            jnp.zeros((owned, LANES - 4 * heads - 1), BF16),
        ],
        1,
    )
    w_shards, w_starts = gathered_shards(packed)
    w_starts = jnp.stack([jnp.asarray(start, jnp.int32) for start in w_starts])
    wo = lax.all_gather(
        flipped(w_out, tuple(w_shards[3:5])), shards, axis=0, tiled=True
    )

    edge, edge_segment = passed_along((hid[rows - EDGE :], segment[rows - 3 :]), "ctx", 1)
    tok = token_marks(segment, edge_segment)
    conv_rows = jnp.concatenate(
        [
            jnp.concatenate([conv_x_w, conv_bc_w.reshape(taps, -1)], 1),
            jnp.concatenate([conv_x_b, conv_bc_b.reshape(-1)])[None],
            jnp.zeros((8 - taps - 1, wide), F32),
        ],
        0,
    )
    spare = jnp.zeros((LANES - 4 * heads,), F32)
    rate = -jnp.exp(a_log)
    dtp = jnp.concatenate(
        [
            jnp.concatenate([dt_bias] * 4 + [spare])[None],
            jnp.concatenate([rate] * 4 + [spare])[None],
            jnp.zeros((6, LANES), F32),
        ],
        0,
    )
    prm = jnp.concatenate(
        [jnp.repeat(skip_d, head_size)[None], out_gain[None], jnp.zeros((6, inner), F32)], 0
    )

    normed, gate, pre, u, rec, st, pdx, state_end, decay_end, w_in, gain = front(
        hid, edge, tok, w_shards, w_starts, 4 * heads, conv_rows, dtp, inner, wide
    )
    sin = chained(state_end, decay_end[:1], "ctx", 1)
    inner_total = inner * lax.axis_size("tp")
    me = lax.axis_index("tp")
    outer = jnp.full((8, LANES), (me == 0) | (me == lax.axis_size("tp") - 1), F32)

    scan, dgate, sums, *parts = middle(u, rec, gate, st, pdx, sin, cot, wo, prm)
    sums, *parts = total_over_row(sums, parts)
    out_sums = [LineSum(part) for part in parts]
    dscan, dgr, glow, adj, psx, adj_start, out_gain_acc = turn(
        scan, gate, dgate, sums, u, rec, prm, inner_total
    )
    ain = chained(adj_start, decay_end[:1], "ctx", -1)
    contract_rows = (((0,), (0,)), ((), ()))
    wo_grad = lax.dot_general(cot, glow, contract_rows, preferred_element_type=F32)

    group_rows = rows // GROUPS
    backs = [None] * GROUPS
    rears = [None] * GROUPS
    d_normed = [None] * GROUPS
    follows = [None] * GROUPS

    def run_back(group, after):
        backs[group] = back(u, rec, dscan, st, pdx, sin, adj, psx, ain, prm, dtp, after, group)
        start = jnp.concatenate(
            [backs[group][0][:8], rec[group * group_rows : group * group_rows + 8]], 1
        )
        if group == 0:
            follows[GROUPS - 1] = passed_along(start, "ctx", -1)
        else:
            follows[group - 1] = start

    def run_rear(group, after):
        rears[group] = rear(
            backs[group][0], rec, pre, dgr, backs[group][1], follows[group], w_in,
            conv_rows, after, group,
        )
        d_normed[group] = LineSum(rears[group][1])

    def settle(group, filled, after=()):
        total = out_sums[group]
        return by_group(
            functools.partial(settle_kernel, float(inner_total)), hid, BF16, group, filled is None,
            [
                (hid, "all"),
                (sums, "columns"),
                (total.given, "group"),
                (total.across, "group"),
                (outer, "whole"),
            ],
            outer if filled is None else filled, after, "settle",
        )

    def finish(group, filled, after):
        total = d_normed[group]
        return by_group(
            finish_kernel, hid, F32, group, filled is None,
            [
                (hid, "all"),
                (cot, "all"),
                (gain, "whole"),
                (total.given, "group"),
                (total.across, "group"),
                (outer, "whole"),
            ],
            outer if filled is None else filled, after, "finish",
        )

    sum_a, sum_b = out_sums
    run_back(0, (wo_grad,))
    done = advance([sum_a], (backs[0][3],))
    run_back(1, done)
    run_rear(0, (backs[1][3],))
    done = advance([sum_b, sum_a], (rears[0][2],))
    run_rear(1, done)

    conv_acc = sum(r[2] for r in rears)
    skip_acc = sum(b[2][0] for b in backs)
    head_acc = sum(b[3] for b in backs)

    dproj = jnp.concatenate([r[0] for r in rears], 0)
    w_grad = lax.dot_general(normed, dproj, contract_rows, preferred_element_type=F32)
    owners = to_owners(w_grad, wo_grad)
    next(owners)
    sum_c, sum_d = d_normed
    done = advance([sum_b], (w_grad[:8, :LANES],))
    block_out = settle(0, None, done)
    done = advance([sum_c], (block_out,))
    owners.send(done)
    done = advance([sum_c], done)
    owners.send(done)
    block_out = settle(1, block_out, done)
    done = advance([sum_d], (block_out,))
    done = advance([sum_d], done)
    hidden_grad = finish(0, None, done)
    owners.send((hidden_grad,))
    both_owned = next(owners)
    hidden_grad = finish(1, hidden_grad, ())
    w_owned, wo_owned = both_owned[:, : w_grad.shape[1]], both_owned[:, w_grad.shape[1] :]

    small = jnp.concatenate(
        [
            conv_acc[: taps + 1].reshape(-1),
            out_gain_acc[0],
            skip_acc,
            head_acc[:2].reshape(-1),
        ]
    )
    small = butterfly_sum(butterfly_sum(small, "ctx"), "fsdp")
    conv_sum = small[: (taps + 1) * wide].reshape(taps + 1, wide)
    rest = small[(taps + 1) * wide :]
    shared = jnp.concatenate(
        [
            w_owned[:, 2 * inner : 2 * inner + 2 * state_size].reshape(-1),
            jnp.sum(packed.astype(F32) * w_owned, 1),
            conv_sum[:, inner:].reshape(-1),
        ]
    )
    shared = butterfly_sum(shared, "tp")
    bc_size = owned * 2 * state_size
    bc_owned = shared[:bc_size].reshape(owned, 2, state_size)
    gain_owned = shared[bc_size : bc_size + owned] / norm_gain.astype(F32)
    conv_bc = shared[bc_size + owned :].reshape(taps + 1, 2, state_size)

    return (
        block_out[None],
        hidden_grad[None],
        gain_owned,
        w_owned[:, : 2 * inner].reshape(owned, 2, inner),
        w_owned[:, 2 * inner + 2 * state_size : 2 * inner + 2 * state_size + heads],
        bc_owned,
        conv_sum[:taps, :inner],
        conv_sum[taps, :inner],
        conv_bc[:taps],
        conv_bc[taps],
        rest[2 * inner : 2 * inner + heads],
        rest[2 * inner + LANES : 2 * inner + LANES + heads],
        jnp.sum(rest[inner : 2 * inner].reshape(heads, head_size), 1),
        rest[:inner],
        wo_owned.T,
    )


def solution(mesh):
    placed = (
        P("fsdp", "ctx", None),
        P("fsdp", "ctx"),
        P("fsdp", "ctx", None),
        P(("fsdp", "ctx")),
        P(("fsdp", "ctx"), None, "tp"),
        P(("fsdp", "ctx"), "tp"),
        P(("fsdp", "ctx"), None, None),
        P(None, "tp"),
        P("tp"),
        P(),
        P(),
        P("tp"),
        P("tp"),
        P("tp"),
        P("tp"),
        P("tp", ("fsdp", "ctx")),
    )
    return jax.shard_map(
        body,
        mesh=mesh,
        in_specs=placed,
        out_specs=(
            P("fsdp", "ctx", None),
            P("fsdp", "ctx", None),
            P(("fsdp", "ctx")),
            P(("fsdp", "ctx"), None, "tp"),
            P(("fsdp", "ctx"), "tp"),
            P(("fsdp", "ctx"), None, None),
            P(None, "tp"),
            P("tp"),
            P(),
            P(),
            P("tp"),
            P("tp"),
            P("tp"),
            P("tp"),
            P("tp", ("fsdp", "ctx")),
        ),
        check_vma=False,
    )
```

profile of v0, /device:TPU:0, one launch (start us, length us, event | category | flops | bytes accessed | tf_op | source)
XLA Modules:
  0.0 462.0 jit_solution(1297015221790466461)
XLA Ops:
  10.9 3.0 collective-permute-start.2
  16.1 2.4 collective-permute-start.1
  26.4 3.6 collective-permute-done.5.refs_4_.refs_2_
  31.3 1.7 flip.1
  39.9 25.6 %front.1 = (bf16[2048,1024]{1,0:T(8,128)(2,1)}, f32[2048,512]{1,0:T(8,128)}, f32[2048,768]{1,0:T(8,128)}, f32[2048,768]{1,0:T(8,128)}, f32[2048,128]{1,0:T(8,128...) custom-call(s32[10]{0:T(128)} %stack.79.starts, ...), custom_call_target="tpu_custom_call" | custom-call | bytes 36900 | tf_op jit(solution)/shard_map/front/pallas_call | solution.py:170
  65.5 2.0 collective-permute-start.11
  69.6 18.4 %middle.1 = (f32[2048,512]{1,0:T(8,128)}, f32[2048,512]{1,0:T(8,128)}, f32[8,2048]{1,0:T(8,128)}, bf16[1024,1024]{1,0:T(8,128)(2,1)}, bf16[1024,1024]{1,0:T(8,128)(2,1)}) custom-call(f32[2048,768]{1,0:T(8,128)} %get-tuple-element.64.u.upre_c.refs_0_, f32[2048,128]{1,0:T(8,128)} %get-tuple-element.65.rec.refs_1_, f32[2048,512]{1,0:T(8,128)} %get-tuple-element.66.gate, ...), custom_call_target="tpu_custom_call" | custom-call | bytes 36900 | tf_op jit(solution)/shard_map/middle/pallas_call | solution.py:289
  88.0 1.7 collective-permute-start.12
  89.7 2.5 collective-permute-start.13
  92.6 4.9 %collective-permute-done.13.two = f32[8,2048]{1,0:T(8,128)S(1)} collective-permute-done((f32[8,2048]{1,0:T(8,128)}, f32[8,2048]{1,0:T(8,128)S(1)}, u32[]{:S(2)}, u32[]{:S(2)}) %collective-permute-start.13) | collective-permute-done | bytes 65568 | tf_op jit(solution)/shard_map/ppermute | solution.py:797
  100.8 4.4 collective-permute-start.16
  105.2 14.2 %turn.1 = (f32[2048,512]{1,0:T(8,128)}, bf16[2048,512]{1,0:T(8,128)(2,1)}, bf16[2048,512]{1,0:T(8,128)(2,1)}, f32[16,128,512]{2,1,0:T(8,128)}, f32[128,512]{1,0:...) custom-call(f32[2048,512]{1,0:T(8,128)} %get-tuple-element.76.scan, f32[2048,512]{1,0:T(8,128)} %get-tuple-element.66.gate, ...), custom_call_target="tpu_custom_call" | custom-call | bytes 36900 | tf_op jit(solution)/shard_map/turn/pallas_call | solution.py:383
  120.7 5.4 %convolution_bitcast_fusion.refs_11_.refs_2_.refs_5_.refs_6_ = f32[1024,512]{1,0:T(8,128)} fusion(bf16[2048,512]{1,0:T(8,128)(2,1)} %get-tuple-element.82, bf16[1,2048,1024]{2,1,0:T(8,128)(2,1)S(1)} %copy-done.1), kind=kOutput, calls=%fused_computation.4 | convolution fusion | flops 2147483648 | bytes 8388608 | tf_op jit(solution)/shard_map/dot_general | solution.py:1046
  126.1 1.6 collective-permute-start.15
  128.5 20.7 %back.2 = (f32[1024,768]{1,0:T(8,128)}, bf16[1024,128]{1,0:T(8,128)(2,1)}, f32[8,512]{1,0:T(8,128)}, f32[8,128]{1,0:T(8,128)}) custom-call(f32[2048,768]{1,0:T(8,128)} %get-tuple-element.64.u.upre_c.refs_0_, f32[2048,128]{1,0:T(8,128)} %get-tuple-element.65.rec.refs_1_, f32[2048,512]{1,0:T(8,128)} %get-tuple-element.78.refs_2_, ...), custom_call_target="tpu_custom_call" | custom-call | bytes 36900 | tf_op jit(solution)/shard_map/back/pallas_call | solution.py:545
  150.2 4.3 join.7.refs_11_.refs_2_
  156.0 20.8 %back.3 = (f32[1024,768]{1,0:T(8,128)}, bf16[1024,128]{1,0:T(8,128)(2,1)}, f32[8,512]{1,0:T(8,128)}, f32[8,128]{1,0:T(8,128)}) custom-call(f32[2048,768]{1,0:T(8,128)} %get-tuple-element.64.u.upre_c.refs_0_, f32[2048,128]{1,0:T(8,128)} %get-tuple-element.65.rec.refs_1_, f32[2048,512]{1,0:T(8,128)} %get-tuple-element.78.refs_2_, ...), custom_call_target="tpu_custom_call" | custom-call | bytes 36900 | tf_op jit(solution)/shard_map/back/pallas_call | solution.py:545
  178.1 11.2 %rear.2 = (bf16[1024,1408]{1,0:T(8,128)(2,1)}, bf16[1024,1024]{1,0:T(8,128)(2,1)}, f32[8,768]{1,0:T(8,128)}) custom-call(f32[1024,768]{1,0:T(8,128)} %get-tuple-element.84.refs_0_, f32[2048,128]{1,0:T(8,128)} %get-tuple-element.65.rec.refs_1_, f32[2048,768]{1,0:T(8,128)} %get-tuple-element.85.refs_2_, bf16[2048,512]{1,0:T(8,128)(2,1)} %get-tuple-element.86.refs_3_, ...), custom_call_target="tpu_custom_call" | custom-call | bytes 36900 | tf_op jit(solution)/shard_map/rear/pallas_call | solution.py:635
  189.2 4.4 collective-permute-done.15.refs_1_
  195.6 5.8 %join.8 = (bf16[1024,1024]{1,0:T(8,128)(2,1)}, bf16[1024,1024]{1,0:T(8,128)(2,1)}) custom-call(bf16[1024,1024]{1,0:T(8,128)(2,1)} %get-tuple-element.74.refs_0_, bf16[1024,1024]{1,0:T(8,128)(2,1)} %copy-done.11, bf16[1024,1024]{1,0:T(8,128)(2,1)} %join.7.refs_11_.refs_2_, bf16[1024,1024]{1,0:T(8,128)(2,1)} %copy-done.12, f32[8,768]{1,0:T(8,128)} %get-tuple-element.91.refs_4_), custom_call_target="tpu_custom_call" | custom-call | bytes 36900 | tf_op jit(solution)/shard_map/join/pallas_call | solution.py:746
  201.4 2.0 collective-permute-start.19
  204.6 13.2 %collective-permute-start.23 = (bf16[1024,1024]{1,0:T(8,128)(2,1)}, bf16[1024,1024]{1,0:T(8,128)(2,1)}, u32[]{:S(2)}, u32[]{:S(2)}) collective-permute-start(bf16[1024,1024]{1,0:T(8,128)(2,1)} %get-tuple-element.98.refs_0_), channel_id=1, source_target_pairs={{0,1},{3,2},{4,5},{7,6},{8,9},{11,10},{12,13},{15,14},{16,17},{19,... | collective-permute-start | bytes 6291464 | tf_op jit(solution)/shard_map/ppermute | solution.py:769
  222.3 11.3 %rear.3 = (bf16[1024,1408]{1,0:T(8,128)(2,1)}, bf16[1024,1024]{1,0:T(8,128)(2,1)}, f32[8,768]{1,0:T(8,128)}) custom-call(f32[1024,768]{1,0:T(8,128)} %get-tuple-element.88.refs_0_, f32[2048,128]{1,0:T(8,128)} %get-tuple-element.65.rec.refs_1_, f32[2048,768]{1,0:T(8,128)} %get-tuple-element.85.refs_2_, bf16[2048,512]{1,0:T(8,128)(2,1)} %get-tuple-element.86.refs_3_, ...), custom_call_target="tpu_custom_call" | custom-call | bytes 36900 | tf_op jit(solution)/shard_map/rear/pallas_call | solution.py:635
  233.6 9.0 %fusion.refs_1_.refs_2_.refs_3_.refs_4_ = f32[1024,1408]{1,0:T(8,128)S(1)} fusion(bf16[2048,1024]{1,0:T(8,128)(2,1)S(1)} %copy-done.41, bf16[1024,1408]{1,0:T(8,128)(2,1)} %get-tuple-element.97, bf16[1024,1408]{1,0:T(8,128)(2,1)} %get-tuple-element.94), kind=kOutput, calls=%fused_computation | convolution fusion | flops 5917114368 | bytes 15728640 | tf_op jit(solution)/shard_map/dot_general | solution.py:1113
  242.7 2.5 copy-done
  245.8 4.3 join.9.refs_6_.refs_3_
  250.1 6.5 %collective-permute-done.22.refs_2_ = bf16[1024,1024]{1,0:T(8,128)(2,1)S(1)} collective-permute-done((bf16[1024,1024]{1,0:T(8,128)(2,1)}, bf16[1024,1024]{1,0:T(8,128)(2,1)S(1)}, u32[]{:S(2)}, u32[]{:S(2)}) %collective-permute-start.22) | collective-permute-done | bytes 2097184 | tf_op jit(solution)/shard_map/ppermute | solution.py:781
  257.9 5.2 %settle.2.refs_2_.refs_5_ = bf16[2048,1024]{1,0:T(8,128)(2,1)} custom-call(bf16[2048,1024]{1,0:T(8,128)(2,1)} %bitcast.70, f32[8,2048]{1,0:T(8,128)} %get-tuple-element.73.sums.refs_1_, bf16[1024,1024]{1,0:T(8,128)(2,1)} %copy-done.10, bf16[1024,1024]{1,0:T(8,128)(2,1)} %get-tuple-element.96.refs_9_.refs_3_, ...), custom_call_target="tpu_custom_call" | custom-call | bytes 36900 | tf_op jit(solution)/shard_map/settle/pallas_call | solution.py:698
  263.1 4.5 join.10.refs_0_.refs_2_.refs_3_
  267.6 2.0 collective-permute-start.24
  270.9 9.7 %collective-permute-start.25 = (bf16[1024,1024]{1,0:T(8,128)(2,1)}, bf16[1024,1024]{1,0:T(8,128)(2,1)}, u32[]{:S(2)}, u32[]{:S(2)}) collective-permute-start(bf16[1024,1024]{1,0:T(8,128)(2,1)} %get-tuple-element.100.refs_0_), channel_id=1, source_target_pairs={{0,1},{3,2},{4,5},{7,6},{8,9},{11,10},{12,13},{15,14},{16,17},{19,... | collective-permute-start | bytes 6291464 | tf_op jit(solution)/shard_map/ppermute | solution.py:769
  281.2 4.8 %other_core.1 = bf16[512,1920]{1,0:T(8,128)(2,1)} custom-call(s32[3]{0:T(128)} %pad_add_fusion.2.refs_0_, f32[1024,1408]{1,0:T(8,128)} %copy-done, f32[1024,512]{1,0:T(8,128)} %convolution_bitcast_fusion.refs_11_.refs_2_.refs_5_.refs_6_, bf16[1024,1024]{1,0:T(8,128)(2,1)} %join.10.refs_0_.refs_2_.refs_3_), custom_call_target="tpu_custom_call" | custom-call | bytes 36900 | tf_op jit(solution)/shard_map/other_core/pallas_call | solution.py:838
  286.0 4.3 join.11.refs_6_.refs_4_.refs_11_
  290.3 26.7 %collective-permute-done.21.refs_2_ = bf16[1024,1024]{1,0:T(8,128)(2,1)} collective-permute-done((bf16[1024,1024]{1,0:T(8,128)(2,1)S(1)}, bf16[1024,1024]{1,0:T(8,128)(2,1)}, u32[]{:S(2)}, u32[]{:S(2)}) %collective-permute-start.21) | collective-permute-done | bytes 2097184 | tf_op jit(solution)/shard_map/ppermute | solution.py:781
  317.0 5.3 %settle.3.refs_2_ = bf16[2048,1024]{1,0:T(8,128)(2,1)} custom-call(bf16[2048,1024]{1,0:T(8,128)(2,1)} %bitcast.71, f32[8,2048]{1,0:T(8,128)} %get-tuple-element.73.sums.refs_1_, bf16[1024,1024]{1,0:T(8,128)(2,1)} %collective-permute-done.21.refs_2_, bf16[1024,1024]{1,0:T(8,128)(2,1)} %join.9.refs_6_.refs_3_, ...), custom_call_target="tpu_custom_call", output_to_operand_aliasing={{}: (5, {})} | custom-call | bytes 36900 | tf_op jit(solution)/shard_map/settle/pallas_call | solution.py:698
  322.3 4.5 join.12.refs_0_.refs_2_
  326.7 2.0 collective-permute-start.26
  332.8 6.6 %split.1 = (f32[256,1024]{1,0:T(8,128)}, bf16[256,1024]{1,0:T(8,128)(2,1)}, f32[256,896]{1,0:T(8,128)}, bf16[256,896]{1,0:T(8,128)(2,1)}) custom-call(s32[3]{0:T(128)} %pad_add_fusion.2.refs_0_, f32[1024,1408]{1,0:T(8,128)} %copy-done, f32[1024,1408]{1,0:T(8,128)} %copy-done, f32[1024,1408]{1,0:T(8,128)} %copy-done, f32[1024,1408]{1,0:T(8,128)} %copy-done, ...), custom_call_target="tpu_custom_call" | custom-call | bytes 36900 | tf_op jit(solution)/shard_map/split/pallas_call | solution.py:838
  344.2 5.2 %collective-permute-done.35 = f32[5120]{0:T(1024)S(1)} collective-permute-done((f32[5120]{0:T(1024)S(1)}, f32[5120]{0:T(1024)S(1)}, u32[]{:S(2)}, u32[]{:S(2)}) %collective-permute-start.35) | collective-permute-done | bytes 20512 | tf_op jit(solution)/shard_map/ppermute | solution.py:731
  350.6 4.4 join.13.refs_7_.refs_4_
  355.0 20.3 %collective-permute-done.28.refs_3_ = bf16[1024,1024]{1,0:T(8,128)(2,1)} collective-permute-done((bf16[1024,1024]{1,0:T(8,128)(2,1)S(1)}, bf16[1024,1024]{1,0:T(8,128)(2,1)}, u32[]{:S(2)}, u32[]{:S(2)}) %collective-permute-start.28) | collective-permute-done | bytes 2097184 | tf_op jit(solution)/shard_map/ppermute | solution.py:781
  375.3 6.6 %finish.2.refs_6_.refs_9_ = f32[2048,1024]{1,0:T(8,128)} custom-call(bf16[2048,1024]{1,0:T(8,128)(2,1)} %bitcast.72, bf16[2048,1024]{1,0:T(8,128)(2,1)} %bitcast.77, f32[8,1024]{1,0:T(8,128)} %get-tuple-element.99.refs_2_, bf16[1024,1024]{1,0:T(8,128)(2,1)} %collective-permute-done.28.refs_3_, bf16[1024,1024]{1,0:T(8,128)(2,1)} %join.11.refs_6_.refs_4_.refs_11_, ...), custom_call_target="tpu_custom_call" | custom-call | bytes 36900 | tf_op jit(solution)/shard_map/finish/pallas_call | solution.py:698
  382.8 3.7 second.1
  393.9 3.9 collective-permute-done.33
  399.1 6.3 %collective-permute-start.37 = (f32[34176]{0:T(1024)S(1)}, f32[34176]{0:T(1024)S(1)}, u32[]{:S(2)}, u32[]{:S(2)}) collective-permute-start(f32[34176]{0:T(1024)S(1)} %pad_maximum_fusion.1), channel_id=1, source_target_pairs={{0,1},{1,0},{2,3},{3,2},{4,5},{5,4},{6,7},{7,6},{8,9},{9,8},{10,11... | collective-permute-start | bytes 410120 | tf_op jit(solution)/shard_map/ppermute | solution.py:731
  405.9 33.8 %collective-permute-done.37 = f32[34176]{0:T(1024)S(1)} collective-permute-done((f32[34176]{0:T(1024)S(1)}, f32[34176]{0:T(1024)S(1)}, u32[]{:S(2)}, u32[]{:S(2)}) %collective-permute-start.37) | collective-permute-done | bytes 136736 | tf_op jit(solution)/shard_map/ppermute | solution.py:731
  442.6 3.7 collective-permute-done.38
  448.6 6.6 %finish.3 = f32[2048,1024]{1,0:T(8,128)} custom-call(bf16[2048,1024]{1,0:T(8,128)(2,1)} %bitcast.73, bf16[2048,1024]{1,0:T(8,128)(2,1)} %bitcast.78, f32[8,1024]{1,0:T(8,128)} %get-tuple-element.99.refs_2_, bf16[1024,1024]{1,0:T(8,128)(2,1)} %collective-permute-done.27.refs_3_, ...), custom_call_target="tpu_custom_call", output_to_operand_aliasing={{}: (6, {})} | custom-call | bytes 36900 | tf_op jit(solution)/shard_map/finish/pallas_call | solution.py:698
  (228 shorter events, 70.1 us)
Async XLA Ops:
  7.2 27.2 %copy-start.23 = (s32[1,2048]{1,0:T(1,128)S(1)}, s32[1,2048]{1,0:T(1,128)}, u32[]{:S(2)}) copy-start(s32[1,2048]{1,0:T(1,128)} %param.17) | copy-start | bytes 24580
  7.2 25.8 %copy-start.38 = (f32[2,128]{1,0:T(2,128)S(1)}, f32[2,128]{1,0:T(2,128)}, u32[]{:S(2)}) copy-start(f32[2,128]{1,0:T(2,128)} %param.26) | copy-start | bytes 3076
  7.2 25.8 %copy-start.35 = (f32[4,2,128]{2,1,0:T(2,128)S(1)}, f32[4,2,128]{2,1,0:T(2,128)}, u32[]{:S(2)}) copy-start(f32[4,2,128]{2,1,0:T(2,128)} %param.25) | copy-start | bytes 12292
  7.2 26.5 %copy-start.34 = (f32[4,512]{1,0:T(4,128)S(1)}, f32[4,512]{1,0:T(4,128)}, u32[]{:S(2)}) copy-start(f32[4,512]{1,0:T(4,128)} %param.23) | copy-start | bytes 24580
  7.2 61.7 %all-gather.2.cloned.1.call-start = ((), (), s32[]{:S(2)}) async-start(), calls=%async_computation | async-start | bytes 1179648 | tf_op jit(solution)/shard_map/all_gather | solution.py:1002
  10.9 28.1 %copy-start.7 = (bf16[128,1408]{1,0:T(8,128)(2,1)}, bf16[128,1408]{1,0:T(8,128)(2,1)S(1)}, u32[]{:S(2)}) copy-start(bf16[128,1408]{1,0:T(8,128)(2,1)S(1)} %concatenate.56.refs_0_) | copy-start | bytes 1081348
  10.9 13.2 %collective-permute-start.2 = (bf16[128,1408]{1,0:T(8,128)(2,1)S(1)}, bf16[128,1408]{1,0:T(8,128)(2,1)S(1)}, u32[]{:S(2)}, u32[]{:S(2)}) collective-permute-start(bf16[128,1408]{1,0:T(8,128)(2,1)S(1)} %concatenate.56.refs_0_), channel_id=1, source_target_pairs={{0,8},{8,0},{16,24},{24,16},{1,9},{9,1},{17,25},{25,17},{2,10},{10... | collective-permute-start | bytes 1081352 | tf_op jit(solution)/shard_map/ppermute | solution.py:943
  13.9 10.7 %collective-permute-start.3 = (bf16[128,1408]{1,0:T(8,128)(2,1)S(1)}, bf16[128,1408]{1,0:T(8,128)(2,1)S(1)}, u32[]{:S(2)}, u32[]{:S(2)}) collective-permute-start(bf16[128,1408]{1,0:T(8,128)(2,1)S(1)} %concatenate.56.refs_0_), channel_id=1, source_target_pairs={{0,16},{8,24},{16,0},{24,8},{1,17},{9,25},{17,1},{25,9},{2,18},{10... | collective-permute-start | bytes 1081352 | tf_op jit(solution)/shard_map/ppermute | solution.py:943
  15.4 23.5 %collective-permute-start.6 = (bf16[128,1408]{1,0:T(8,128)(2,1)S(1)}, bf16[128,1408]{1,0:T(8,128)(2,1)S(1)}, u32[]{:S(2)}, u32[]{:S(2)}) collective-permute-start(bf16[128,1408]{1,0:T(8,128)(2,1)S(1)} %concatenate.56.refs_0_), channel_id=1, source_target_pairs={{0,4},{4,0},{1,5},{5,1},{2,6},{6,2},{3,7},{7,3},{8,12},{12,8},{9,1... | collective-permute-start | bytes 1081352 | tf_op jit(solution)/shard_map/ppermute | solution.py:943
  16.1 18.3 %collective-permute-start.1 = (s32[3]{0:T(128)S(1)}, s32[3]{0:T(128)S(1)}, u32[]{:S(2)}, u32[]{:S(2)}) collective-permute-start(s32[3]{0:T(128)S(1)} %slice_bitcast_fusion.5), channel_id=1, source_target_pairs={{0,4},{1,5},{2,6},{3,7},{8,12},{9,13},{10,14},{11,15},{16,20},{17,... | collective-permute-start | bytes 44 | tf_op jit(solution)/shard_map/ppermute | solution.py:716
  19.3 17.2 %collective-permute-start = (bf16[16,1024]{1,0:T(8,128)(2,1)S(1)}, bf16[16,1024]{1,0:T(8,128)(2,1)S(1)}, u32[]{:S(2)}, u32[]{:S(2)}) collective-permute-start(bf16[16,1024]{1,0:T(8,128)(2,1)S(1)} %slice_bitcast_fusion.2), channel_id=1, source_target_pairs={{0,4},{1,5},{2,6},{3,7},{8,12},{9,13},{10,14},{11,15},{16,20},{17,... | collective-permute-start | bytes 98312 | tf_op jit(solution)/shard_map/ppermute | solution.py:716
  24.0 5.9 %collective-permute-start.5 = (bf16[64,1408]{1,0:T(8,128)(2,1)S(1)}, bf16[64,1408]{1,0:T(8,128)(2,1)S(1)}, u32[]{:S(2)}, u32[]{:S(2)}) collective-permute-start(bf16[64,1408]{1,0:T(8,128)(2,1)S(1)} %slice.204), channel_id=1, source_target_pairs={{0,16},{8,24},{16,0},{24,8},{1,17},{9,25},{17,1},{25,9},{2,18},{10... | collective-permute-start | bytes 540680 | tf_op jit(solution)/shard_map/ppermute | solution.py:943
  24.6 5.6 %collective-permute-start.4 = (bf16[64,1408]{1,0:T(8,128)(2,1)S(1)}, bf16[64,1408]{1,0:T(8,128)(2,1)S(1)}, u32[]{:S(2)}, u32[]{:S(2)}) collective-permute-start(bf16[64,1408]{1,0:T(8,128)(2,1)S(1)} %slice.203), channel_id=1, source_target_pairs={{0,8},{8,0},{16,24},{24,16},{1,9},{9,1},{17,25},{25,17},{2,10},{10... | collective-permute-start | bytes 540680 | tf_op jit(solution)/shard_map/ppermute | solution.py:943
  35.7 3.2 collective-permute-start.7
  35.7 3.2 collective-permute-start.8
  36.4 2.5 collective-permute-start.10
  36.5 2.4 collective-permute-start.9
  39.9 27.7 %copy-start.40 = (f32[8]{0:T(128)S(1)}, f32[8]{0:T(128)}, u32[]{:S(2)}) copy-start(f32[8]{0:T(128)} %param.29) | copy-start | bytes 100
  39.9 27.8 %copy-start.37 = (f32[512]{0:T(512)S(1)}, f32[512]{0:T(512)}, u32[]{:S(2)}) copy-start(f32[512]{0:T(512)} %param.30) | copy-start | bytes 6148
  65.5 3.4 collective-permute-start.11
  88.0 4.6 %collective-permute-start.12 = (f32[8,2048]{1,0:T(8,128)}, f32[8,2048]{1,0:T(8,128)S(1)}, u32[]{:S(2)}, u32[]{:S(2)}) collective-permute-start(f32[8,2048]{1,0:T(8,128)} %get-tuple-element.70.own), channel_id=1, source_target_pairs={{0,1},{1,0},{2,3},{3,2},{4,5},{5,4},{6,7},{7,6},{8,9},{9,8},{10,11... | collective-permute-start | bytes 196616 | tf_op jit(solution)/shard_map/ppermute | solution.py:797
  89.7 7.9 %collective-permute-start.13 = (f32[8,2048]{1,0:T(8,128)}, f32[8,2048]{1,0:T(8,128)S(1)}, u32[]{:S(2)}, u32[]{:S(2)}) collective-permute-start(f32[8,2048]{1,0:T(8,128)} %get-tuple-element.70.own), channel_id=1, source_target_pairs={{0,2},{1,3},{2,0},{3,1},{4,6},{5,7},{6,4},{7,5},{8,10},{9,11},{10,... | collective-permute-start | bytes 196616 | tf_op jit(solution)/shard_map/ppermute | solution.py:797
  92.2 6.3 %collective-permute-start.14 = (f32[8,2048]{1,0:T(8,128)}, f32[8,2048]{1,0:T(8,128)S(1)}, u32[]{:S(2)}, u32[]{:S(2)}) collective-permute-start(f32[8,2048]{1,0:T(8,128)} %get-tuple-element.70.own), channel_id=1, source_target_pairs={{0,3},{1,2},{2,1},{3,0},{4,7},{5,6},{6,5},{7,4},{8,11},{9,10},{10,... | collective-permute-start | bytes 196616 | tf_op jit(solution)/shard_map/ppermute | solution.py:797
  100.8 49.4 %collective-permute-start.16 = (bf16[1024,1024]{1,0:T(8,128)(2,1)}, bf16[1024,1024]{1,0:T(8,128)(2,1)}, u32[]{:S(2)}, u32[]{:S(2)}) collective-permute-start(bf16[1024,1024]{1,0:T(8,128)(2,1)} %get-tuple-element.75.refs_0_), channel_id=1, source_target_pairs={{0,1},{3,2},{4,5},{7,6},{8,9},{11,10},{12,13},{15,14},{16,17},{19,... | collective-permute-start | bytes 6291464 | tf_op jit(solution)/shard_map/ppermute | solution.py:769
  119.4 8.3 %collective-permute-start.17 = (f32[128,512]{1,0:T(8,128)}, f32[128,512]{1,0:T(8,128)S(1)}, u32[]{:S(2)}, u32[]{:S(2)}) collective-permute-start(f32[128,512]{1,0:T(8,128)} %get-tuple-element.81), channel_id=1, source_target_pairs={{4,0},{5,1},{6,2},{7,3},{12,8},{13,9},{14,10},{15,11},{20,16},{21,... | collective-permute-start | bytes 786440 | tf_op jit(solution)/shard_map/ppermute | solution.py:716
  126.1 67.5 %collective-permute-start.15 = (bf16[1024,1024]{1,0:T(8,128)(2,1)S(1)}, bf16[1024,1024]{1,0:T(8,128)(2,1)S(1)}, u32[]{:S(2)}, u32[]{:S(2)}) collective-permute-start(bf16[1024,1024]{1,0:T(8,128)(2,1)S(1)} %copy-done.6), channel_id=1, source_target_pairs={{0,1},{3,2},{4,5},{7,6},{8,9},{11,10},{12,13},{15,14},{16,17},{19,... | collective-permute-start | bytes 6291464 | tf_op jit(solution)/shard_map/ppermute | solution.py:769
  154.5 39.1 %collective-permute-start.18 = (bf16[1024,1024]{1,0:T(8,128)(2,1)}, bf16[1024,1024]{1,0:T(8,128)(2,1)S(1)}, u32[]{:S(2)}, u32[]{:S(2)}) collective-permute-start(bf16[1024,1024]{1,0:T(8,128)(2,1)} %join.7.refs_11_.refs_2_), channel_id=1, source_target_pairs={{1,2},{2,1},{5,6},{6,5},{9,10},{10,9},{13,14},{14,13},{17,18},{18,... | collective-permute-start | bytes 6291464 | tf_op jit(solution)/shard_map/ppermute | solution.py:778
  201.4 44.4 %collective-permute-start.19 = (bf16[1024,1024]{1,0:T(8,128)(2,1)}, bf16[1024,1024]{1,0:T(8,128)(2,1)}, u32[]{:S(2)}, u32[]{:S(2)}) collective-permute-start(bf16[1024,1024]{1,0:T(8,128)(2,1)} %get-tuple-element.92.refs_8_.refs_0_), channel_id=1, source_target_pairs={{1,2},{2,1},{5,6},{6,5},{9,10},{10,9},{13,14},{14,13},{17,18},{18,... | collective-permute-start | bytes 6291464 | tf_op jit(solution)/shard_map/ppermute | solution.py:778
  203.3 53.2 %collective-permute-start.22 = (bf16[1024,1024]{1,0:T(8,128)(2,1)}, bf16[1024,1024]{1,0:T(8,128)(2,1)S(1)}, u32[]{:S(2)}, u32[]{:S(2)}) collective-permute-start(bf16[1024,1024]{1,0:T(8,128)(2,1)} %get-tuple-element.96.refs_9_.refs_3_), channel_id=1, source_target_pairs={{1,0},{2,3},{5,4},{6,7},{9,8},{10,11},{13,12},{14,15},{17,16},{18,... | collective-permute-start | bytes 6291464 | tf_op jit(solution)/shard_map/ppermute | solution.py:781
  204.6 58.5 %collective-permute-start.23 = (bf16[1024,1024]{1,0:T(8,128)(2,1)}, bf16[1024,1024]{1,0:T(8,128)(2,1)}, u32[]{:S(2)}, u32[]{:S(2)}) collective-permute-start(bf16[1024,1024]{1,0:T(8,128)(2,1)} %get-tuple-element.98.refs_0_), channel_id=1, source_target_pairs={{0,1},{3,2},{4,5},{7,6},{8,9},{11,10},{12,13},{15,14},{16,17},{19,... | collective-permute-start | bytes 6291464 | tf_op jit(solution)/shard_map/ppermute | solution.py:769
  218.6 3.1 collective-permute-start.20
  267.6 18.3 %collective-permute-start.24 = (bf16[1024,1024]{1,0:T(8,128)(2,1)}, bf16[1024,1024]{1,0:T(8,128)(2,1)}, u32[]{:S(2)}, u32[]{:S(2)}) collective-permute-start(bf16[1024,1024]{1,0:T(8,128)(2,1)} %join.10.refs_0_.refs_2_.refs_3_), channel_id=1, source_target_pairs={{1,2},{2,1},{5,6},{6,5},{9,10},{10,9},{13,14},{14,13},{17,18},{18,... | collective-permute-start | bytes 6291464 | tf_op jit(solution)/shard_map/ppermute | solution.py:778
  269.6 47.4 %collective-permute-start.21 = (bf16[1024,1024]{1,0:T(8,128)(2,1)S(1)}, bf16[1024,1024]{1,0:T(8,128)(2,1)}, u32[]{:S(2)}, u32[]{:S(2)}) collective-permute-start(bf16[1024,1024]{1,0:T(8,128)(2,1)S(1)} %copy-done.5), channel_id=1, source_target_pairs={{1,0},{2,3},{5,4},{6,7},{9,8},{10,11},{13,12},{14,15},{17,16},{18,... | collective-permute-start | bytes 6291464 | tf_op jit(solution)/shard_map/ppermute | solution.py:781
  270.9 51.4 %collective-permute-start.25 = (bf16[1024,1024]{1,0:T(8,128)(2,1)}, bf16[1024,1024]{1,0:T(8,128)(2,1)}, u32[]{:S(2)}, u32[]{:S(2)}) collective-permute-start(bf16[1024,1024]{1,0:T(8,128)(2,1)} %get-tuple-element.100.refs_0_), channel_id=1, source_target_pairs={{0,1},{3,2},{4,5},{7,6},{8,9},{11,10},{12,13},{15,14},{16,17},{19,... | collective-permute-start | bytes 6291464 | tf_op jit(solution)/shard_map/ppermute | solution.py:769
  285.9 45.6 %collective-permute-start.29 = (bf16[512,1920]{1,0:T(8,128)(2,1)}, bf16[512,1920]{1,0:T(8,128)(2,1)S(1)}, u32[]{:S(2)}, u32[]{:S(2)}) collective-permute-start(bf16[512,1920]{1,0:T(8,128)(2,1)} %other_core.1), channel_id=1, source_target_pairs={{0,4},{4,0},{1,5},{5,1},{2,6},{6,2},{3,7},{7,3},{8,12},{12,8},{9,1... | collective-permute-start | bytes 5898248 | tf_op jit(solution)/shard_map/ppermute | solution.py:873
  326.7 23.9 %collective-permute-start.26 = (bf16[1024,1024]{1,0:T(8,128)(2,1)}, bf16[1024,1024]{1,0:T(8,128)(2,1)}, u32[]{:S(2)}, u32[]{:S(2)}) collective-permute-start(bf16[1024,1024]{1,0:T(8,128)(2,1)} %join.12.refs_0_.refs_2_), channel_id=1, source_target_pairs={{1,2},{2,1},{5,6},{6,5},{9,10},{10,9},{13,14},{14,13},{17,18},{18,... | collective-permute-start | bytes 6291464 | tf_op jit(solution)/shard_map/ppermute | solution.py:778
  328.7 46.6 %collective-permute-start.28 = (bf16[1024,1024]{1,0:T(8,128)(2,1)S(1)}, bf16[1024,1024]{1,0:T(8,128)(2,1)}, u32[]{:S(2)}, u32[]{:S(2)}) collective-permute-start(bf16[1024,1024]{1,0:T(8,128)(2,1)S(1)} %copy-done.2), channel_id=1, source_target_pairs={{1,0},{2,3},{5,4},{6,7},{9,8},{10,11},{13,12},{14,15},{17,16},{18,... | collective-permute-start | bytes 6291464 | tf_op jit(solution)/shard_map/ppermute | solution.py:781
  339.4 42.4 %collective-permute-start.30 = (bf16[256,1024]{1,0:T(8,128)(2,1)}, bf16[256,1024]{1,0:T(8,128)(2,1)S(1)}, u32[]{:S(2)}, u32[]{:S(2)}) collective-permute-start(bf16[256,1024]{1,0:T(8,128)(2,1)} %get-tuple-element.102), channel_id=1, source_target_pairs={{0,8},{8,0},{16,24},{24,16},{1,9},{9,1},{17,25},{25,17},{2,10},{10... | collective-permute-start | bytes 1572872 | tf_op jit(solution)/shard_map/ppermute | solution.py:873
  340.2 41.6 %collective-permute-start.31 = (bf16[256,896]{1,0:T(8,128)(2,1)}, bf16[256,896]{1,0:T(8,128)(2,1)S(1)}, u32[]{:S(2)}, u32[]{:S(2)}) collective-permute-start(bf16[256,896]{1,0:T(8,128)(2,1)} %get-tuple-element.104), channel_id=1, source_target_pairs={{0,16},{8,24},{16,0},{24,8},{1,17},{9,25},{17,1},{25,9},{2,18},{10... | collective-permute-start | bytes 1376264 | tf_op jit(solution)/shard_map/ppermute | solution.py:873
  341.3 1.3 collective-permute-start.34
  342.6 6.7 %collective-permute-start.35 = (f32[5120]{0:T(1024)S(1)}, f32[5120]{0:T(1024)S(1)}, u32[]{:S(2)}, u32[]{:S(2)}) collective-permute-start(f32[5120]{0:T(1024)S(1)} %fusion.22), channel_id=1, source_target_pairs={{0,8},{8,0},{16,24},{24,16},{1,9},{9,1},{17,25},{25,17},{2,10},{10... | collective-permute-start | bytes 61448 | tf_op jit(solution)/shard_map/ppermute | solution.py:731
  349.3 38.0 %collective-permute-start.36 = (f32[5120]{0:T(1024)S(1)}, f32[5120]{0:T(1024)S(1)}, u32[]{:S(2)}, u32[]{:S(2)}) collective-permute-start(f32[5120]{0:T(1024)S(1)} %add.90), channel_id=1, source_target_pairs={{0,16},{8,24},{16,0},{24,8},{1,17},{9,25},{17,1},{25,9},{2,18},{10... | collective-permute-start | bytes 61448 | tf_op jit(solution)/shard_map/ppermute | solution.py:731
  386.5 6.2 %collective-permute-start.32 = (bf16[128,896]{1,0:T(8,128)(2,1)}, bf16[128,896]{1,0:T(8,128)(2,1)S(1)}, u32[]{:S(2)}, u32[]{:S(2)}) collective-permute-start(bf16[128,896]{1,0:T(8,128)(2,1)} %get-tuple-element.106), channel_id=1, source_target_pairs={{0,8},{8,0},{16,24},{24,16},{1,9},{9,1},{17,25},{25,17},{2,10},{10... | collective-permute-start | bytes 688136 | tf_op jit(solution)/shard_map/ppermute | solution.py:873
  389.8 58.8 %collective-permute-start.27 = (bf16[1024,1024]{1,0:T(8,128)(2,1)S(1)}, bf16[1024,1024]{1,0:T(8,128)(2,1)}, u32[]{:S(2)}, u32[]{:S(2)}) collective-permute-start(bf16[1024,1024]{1,0:T(8,128)(2,1)S(1)} %copy-done.4), channel_id=1, source_target_pairs={{1,0},{2,3},{5,4},{6,7},{9,8},{10,11},{13,12},{14,15},{17,16},{18,... | collective-permute-start | bytes 6291464 | tf_op jit(solution)/shard_map/ppermute | solution.py:781
  391.1 6.6 %collective-permute-start.33 = (bf16[128,1024]{1,0:T(8,128)(2,1)}, bf16[128,1024]{1,0:T(8,128)(2,1)S(1)}, u32[]{:S(2)}, u32[]{:S(2)}) collective-permute-start(bf16[128,1024]{1,0:T(8,128)(2,1)} %get-tuple-element.108), channel_id=1, source_target_pairs={{0,16},{8,24},{16,0},{24,8},{1,17},{9,25},{17,1},{25,9},{2,18},{10... | collective-permute-start | bytes 786440 | tf_op jit(solution)/shard_map/ppermute | solution.py:873
  397.8 50.3 %copy-start.39 = (bf16[128]{0:T(256)(128)(2,1)S(1)}, bf16[128]{0:T(256)(128)(2,1)}, u32[]{:S(2)}) copy-start(bf16[128]{0:T(256)(128)(2,1)} %param.19) | copy-start | bytes 772
  399.1 40.6 %collective-permute-start.37 = (f32[34176]{0:T(1024)S(1)}, f32[34176]{0:T(1024)S(1)}, u32[]{:S(2)}, u32[]{:S(2)}) collective-permute-start(f32[34176]{0:T(1024)S(1)} %pad_maximum_fusion.1), channel_id=1, source_target_pairs={{0,1},{1,0},{2,3},{3,2},{4,5},{5,4},{6,7},{7,6},{8,9},{9,8},{10,11... | collective-permute-start | bytes 410120 | tf_op jit(solution)/shard_map/ppermute | solution.py:731
  439.7 6.5 %collective-permute-start.38 = (f32[34176]{0:T(1024)S(1)}, f32[34176]{0:T(1024)S(1)}, u32[]{:S(2)}, u32[]{:S(2)}) collective-permute-start(f32[34176]{0:T(1024)S(1)} %fusion.21), channel_id=1, source_target_pairs={{0,2},{1,3},{2,0},{3,1},{4,6},{5,7},{6,4},{7,5},{8,10},{9,11},{10,... | collective-permute-start | bytes 410120 | tf_op jit(solution)/shard_map/ppermute | solution.py:731
  (34 other events, 183.3 us)
Sparse Core Ops, SparseCore 0:
  33.1 23.4 all-gather.1
where the time goes:
time: 464 us; the launch traced here: 462 us
  Pallas kernels  196 us (42%)
  waiting for transfers between devices  119 us (26%)
  starting transfers between devices  74.1 us (16%)
  local copies, waits for them, and re-layouts  34.4 us (7%)
  between operations  14.7 us (3%)
  matrix products  14.4 us (3%)
  other arithmetic  9.01 us (2%)
    ppermute x4, waiting for transfers between devices, joined(): self.given = lax.ppermute(value, 'tp', [(1, 0), (2, 3)])  53.5 us
    ppermute x5, waiting for transfers between devices, butterfly_sum(): value = value + lax.ppermute(value, axis, pairs)  43.8 us
    pallas_call x2, Pallas kernels, back(): pl.pallas_call(ordered(back_kernel, 11, len(after)), grid=(steps,), in_sp...  41.5 us
    pallas_call x7, Pallas kernels, join(): pl.pallas_call(ordered(functools.partial(join_kernel, len(pairs)), 2 * le...  32.1 us
    ppermute x4, starting transfers between devices, __init__(): self.come = lax.ppermute(value, 'tp', [(0, 1), (3, 2)])  29 us
    pallas_call x1, Pallas kernels, front(): pl.pallas_call(functools.partial(front_kernel, gain_lane), grid=(steps,),...  25.6 us
    pallas_call x4, Pallas kernels, by_group(): pl.pallas_call(ordered(kernel, count, len(after)), grid=(steps,), in_spec...  23.7 us
    pallas_call x2, Pallas kernels, rear(): pl.pallas_call(ordered(rear_kernel, 8, len(after)), grid=(steps,), in_spe...  22.5 us
  transfers between devices with their start and end apart: 40, of which 18 were waited for; matrix products, arithmetic and copies ran while one was open for 9% of the time, Pallas kernels for 35%

commit v1 on v0

--- a/solution.py
+++ b/solution.py
@@ -668,14 +668,14 @@
     )(dpre, rec, pre, dgr, dstep, follow, w, cw, *after)
 
 
-def settle_kernel(inner_total, hid, sums, given, held, outer, filled, out):
+def settle_kernel(inner_total, hid, sums, given, held, outer, filled, out, *handed):
     column = jnp.concatenate([sums[...], jnp.zeros((LANES - 8, STEP), F32)], 0).T
     inv = lax.rsqrt(column[:, 0:1] / inner_total + EPSILON)
     total = jnp.where(outer[0:1, 0:1] > 0.0, given[...].astype(F32), held[...].astype(F32))
     out[...] = (hid[...].astype(F32) + inv * total).astype(BF16)
 
 
-def finish_kernel(hid, cot, gain, given, held, outer, filled, out):
+def finish_kernel(hid, cot, gain, given, held, outer, filled, out, *handed):
     x = hid[...].astype(F32)
     inv = lax.rsqrt(jnp.mean(x * x, -1, keepdims=True) + EPSILON)
     total = jnp.where(outer[0:1, 0:1] > 0.0, given[...].astype(F32), held[...].astype(F32))
@@ -684,7 +684,7 @@
     out[...] = cot[...].astype(F32) + inv * scaled - x * (inv * inv * inv * cross)
 
 
-def by_group(kernel, out_like, dtype, group, fresh, operands, filled, after, name):
+def by_group(kernel, out_like, dtype, group, fresh, operands, filled, after, name, held=()):
     rows, width = out_like.shape
     steps = rows // GROUPS // STEP
     first = group * steps
@@ -695,19 +695,25 @@
         "whole": lambda a: pl.BlockSpec(a.shape, lambda i: (0, 0)),
     }
     count = len(operands) + 1
-    return pl.pallas_call(
-        ordered(kernel, count, len(after)),
+    aliases = {} if fresh else {count - 1: 0}
+    aliases.update({count + len(after) + k: 1 + k for k in range(len(held))})
+    out, *handed = pl.pallas_call(
+        ordered(kernel, count, len(after) + len(held)),
         grid=(steps,),
-        in_specs=[specs[kind](a) for a, kind in operands] + [ANYWHERE] * (1 + len(after)),
-        out_specs=pl.BlockSpec((STEP, width), lambda i: (first + i, 0)),
-        out_shape=jax.ShapeDtypeStruct((rows, width), dtype),
-        input_output_aliases={} if fresh else {count - 1: 0},
+        in_specs=[specs[kind](a) for a, kind in operands]
+        + [ANYWHERE] * (1 + len(after) + len(held)),
+        out_specs=[pl.BlockSpec((STEP, width), lambda i: (first + i, 0))]
+        + [ANYWHERE] * len(held),
+        out_shape=[jax.ShapeDtypeStruct((rows, width), dtype)]
+        + [jax.ShapeDtypeStruct(a.shape, a.dtype) for a in held],
+        input_output_aliases=aliases,
         compiler_params=pltpu.CompilerParams(
             dimension_semantics=("arbitrary",), vmem_limit_bytes=VMEM_LIMIT
         ),
         cost_estimate=lasts(0.01),
         name=name,
-    )(*[a for a, _ in operands], filled, *after)
+    )(*[a for a, _ in operands], filled, *after, *held)
+    return (out, handed) if held else out
 
 
 def passed_along(value, axis, steps):
@@ -763,10 +769,39 @@
     )(*[a for pair in pairs for a in pair], *after, *held)
 
 
+def trade_kernel(pairs, *refs):
+    own, outer = refs[2 * pairs], refs[2 * pairs + 1]
+    outs = refs[2 * pairs + 2 :]
+    for k in range(pairs):
+        left, right = refs[2 * k], refs[2 * k + 1]
+        total = left[...].astype(F32) + right[...].astype(F32)
+        outs[k][...] = total.astype(BF16)
+    outs[pairs][...] = jnp.where(outer[0:1, 0:1] > 0.0, own[...].astype(F32), total).astype(BF16)
+
+
+def trade(pairs, own, outer, after):
+    rows, width = own.shape
+    spec = pl.BlockSpec((STEP, width), lambda i: (i, 0))
+    flag = pl.BlockSpec(outer.shape, lambda i: (0, 0))
+    count = len(pairs)
+    return pl.pallas_call(
+        ordered(functools.partial(trade_kernel, count), 2 * count + 2, len(after)),
+        grid=(rows // STEP,),
+        in_specs=[spec] * (2 * count + 1) + [flag] + [ANYWHERE] * len(after),
+        out_specs=[spec] * (count + 1),
+        out_shape=[jax.ShapeDtypeStruct((rows, width), BF16)] * (count + 1),
+        compiler_params=pltpu.CompilerParams(
+            dimension_semantics=("arbitrary",), vmem_limit_bytes=VMEM_LIMIT
+        ),
+        cost_estimate=lasts(0.01),
+        name="trade",
+    )(*[a for pair in pairs for a in pair], own, outer, *after)
+
+
 class LineSum:
-    def __init__(self, value):
+    def __init__(self, value, come=None):
         self.own = value
-        self.come = lax.ppermute(value, "tp", [(0, 1), (3, 2)])
+        self.come = lax.ppermute(value, "tp", [(0, 1), (3, 2)]) if come is None else come
         self.near = self.across = self.given = None
 
     def pair(self):
@@ -779,6 +814,16 @@
         else:
             self.across = value
             self.given = lax.ppermute(value, "tp", [(1, 0), (2, 3)])
+
+
+def advance_and_begin(sums, value, outer, after):
+    *outs, both = trade([one.pair() for one in sums], value, outer, after)
+    for one, out in zip(sums[:-1], outs):
+        one.joined(out)
+    sums[-1].across = outs[-1]
+    come = lax.ppermute(both, "tp", [(0, 1), (1, 0), (2, 3), (3, 2)])
+    sums[-1].given = come
+    return LineSum(value, come), tuple(outs)
 
 
 def advance(sums, after, held=()):
@@ -864,7 +909,7 @@
         summed = lax.psum_scatter(both, ("fsdp", "ctx"), scatter_dimension=0, tiled=True)
         yield w
         yield w
-        yield w
+        (summed,) = yield w, [summed]
         yield summed
         return
 
@@ -912,7 +957,7 @@
         [(cut, F32), (cut, BF16), (rest, F32), (rest, BF16)], "second", after,
     )
     come_a, come_b = swapped(send_a, "fsdp", 2), swapped(send_b, "fsdp", 1)
-    yield send_a
+    keep_a, keep_b = yield send_a, [keep_a, keep_b]
     yield jnp.concatenate([keep_a + come_a.astype(F32), keep_b + come_b.astype(F32)], 1)
 
 
@@ -1066,7 +1111,6 @@
             backs[group][0], rec, pre, dgr, backs[group][1], follows[group], w_in,
             conv_rows, after, group,
         )
-        d_normed[group] = LineSum(rears[group][1])
 
     def settle(group, filled, after=()):
         total = out_sums[group]
@@ -1082,7 +1126,7 @@
             outer if filled is None else filled, after, "settle",
         )
 
-    def finish(group, filled, after):
+    def finish(group, filled, after, held=()):
         total = d_normed[group]
         return by_group(
             finish_kernel, hid, F32, group, filled is None,
@@ -1094,7 +1138,7 @@
                 (total.across, "group"),
                 (outer, "whole"),
             ],
-            outer if filled is None else filled, after, "finish",
+            outer if filled is None else filled, after, "finish", held,
         )
 
     sum_a, sum_b = out_sums
@@ -1102,7 +1146,7 @@
     done = advance([sum_a], (backs[0][3],))
     run_back(1, done)
     run_rear(0, (backs[1][3],))
-    done = advance([sum_b, sum_a], (rears[0][2],))
+    d_normed[0], done = advance_and_begin([sum_b, sum_a], rears[0][1], outer, (rears[0][2],))
     run_rear(1, done)
 
     conv_acc = sum(r[2] for r in rears)
@@ -1113,19 +1157,21 @@
     w_grad = lax.dot_general(normed, dproj, contract_rows, preferred_element_type=F32)
     owners = to_owners(w_grad, wo_grad)
     next(owners)
+    d_normed[1], done = advance_and_begin(
+        [sum_b], rears[1][1], outer, (w_grad[:8, :LANES],)
+    )
     sum_c, sum_d = d_normed
-    done = advance([sum_b], (w_grad[:8, :LANES],))
     block_out = settle(0, None, done)
     done = advance([sum_c], (block_out,))
     owners.send(done)
     done = advance([sum_c], done)
-    owners.send(done)
-    block_out = settle(1, block_out, done)
+    sent = owners.send(done)
+    block_out = settle(1, block_out, done + (sent,))
     done = advance([sum_d], (block_out,))
-    done = advance([sum_d], done)
-    hidden_grad = finish(0, None, done)
-    owners.send((hidden_grad,))
-    both_owned = next(owners)
+    sent, kept = owners.send(done)
+    done = advance([sum_d], (sent,))
+    hidden_grad, kept = finish(0, None, done, kept)
+    both_owned = owners.send(kept)
     hidden_grad = finish(1, hidden_grad, ())
     w_owned, wo_owned = both_owned[:, : w_grad.shape[1]], both_owned[:, w_grad.shape[1] :]
 

time: 464 us -> 463 us (level)
    ppermute x4, waiting for transfers between devices: 5.35 us -> 33.2 us  [the longest x2 30.3 us: advance_and_begin(): come = lax.ppermute(both, 'tp', [(0, 1), (1, 0), (2, 3), (3, 2)])]
    ppermute x4 -> x2, waiting for transfers between devices: 53.5 us -> 27.6 us  [joined(): self.given = lax.ppermute(value, 'tp', [(1, 0), (2, 3)])]
    pallas_call x4 -> x6, Pallas kernels: 23.7 us -> 36.7 us  [the longest x4 23.6 us: by_group(): pl.pallas_call(ordered(kernel, count, len(after) + len(held)), grid=(step...]
    pallas_call x7 -> x5, Pallas kernels: 32.1 us -> 21.9 us  [join(): pl.pallas_call(ordered(functools.partial(join_kernel, len(pairs)), 2 * le...]
    unnamed x94 -> x90, local copies, waits for them, and re-layouts: 16.5 us -> 17.7 us
  transfers between devices with their start and end apart: 40 -> 38, of which waited for: 18 -> 15; matrix products, arithmetic and copies ran while one was open for 9% -> 9% of each run, Pallas kernels for 35% -> 32%
where the time goes in v1:
time: 463 us; the launch traced here: 461 us
  Pallas kernels  199 us (43%)
  waiting for transfers between devices  116 us (25%)
  starting transfers between devices  71 us (15%)
  local copies, waits for them, and re-layouts  35.6 us (8%)
  matrix products  14.9 us (3%)
  between operations  14.7 us (3%)
  other arithmetic  9.04 us (2%)
    ppermute x5, waiting for transfers between devices, butterfly_sum(): value = value + lax.ppermute(value, axis, pairs)  43.1 us
    pallas_call x2, Pallas kernels, back(): pl.pallas_call(ordered(back_kernel, 11, len(after)), grid=(steps,), in_sp...  41.5 us
    ppermute x2, waiting for transfers between devices, advance_and_begin(): come = lax.ppermute(both, 'tp', [(0, 1), (1, 0), (2, 3), (3, 2)])  30.3 us
    ppermute x2, waiting for transfers between devices, joined(): self.given = lax.ppermute(value, 'tp', [(1, 0), (2, 3)])  27.6 us
    pallas_call x1, Pallas kernels, front(): pl.pallas_call(functools.partial(front_kernel, gain_lane), grid=(steps,),...  25.7 us
    pallas_call x4, Pallas kernels, by_group(): pl.pallas_call(ordered(kernel, count, len(after) + len(held)), grid=(step...  23.6 us
    pallas_call x2, Pallas kernels, rear(): pl.pallas_call(ordered(rear_kernel, 8, len(after)), grid=(steps,), in_spe...  22.5 us
    pallas_call x5, Pallas kernels, join(): pl.pallas_call(ordered(functools.partial(join_kernel, len(pairs)), 2 * le...  21.9 us
  transfers between devices with their start and end apart: 38, of which 15 were waited for; matrix products, arithmetic and copies ran while one was open for 9% of the time, Pallas kernels for 32%

profile of v1, /device:TPU:0, one launch (start us, length us, event | category | flops | bytes accessed | tf_op | source)
XLA Modules:
  0.0 460.6 jit_solution(8097948345496976378)
XLA Ops:
  10.9 3.0 collective-permute-start.2
  16.1 2.4 collective-permute-start.1
  26.4 3.6 collective-permute-done.5.refs_4_.refs_2_
  31.3 1.7 flip.1
  39.9 25.7 %front.1 = (bf16[2048,1024]{1,0:T(8,128)(2,1)}, f32[2048,512]{1,0:T(8,128)}, f32[2048,768]{1,0:T(8,128)}, f32[2048,768]{1,0:T(8,128)}, f32[2048,128]{1,0:T(8,128...) custom-call(s32[10]{0:T(128)} %stack.79.starts, ...), custom_call_target="tpu_custom_call" | custom-call | bytes 36900 | tf_op jit(solution)/shard_map/front/pallas_call | solution.py:170
  65.6 2.0 collective-permute-start.11
  69.6 18.4 %middle.1 = (f32[2048,512]{1,0:T(8,128)}, f32[2048,512]{1,0:T(8,128)}, f32[8,2048]{1,0:T(8,128)}, bf16[1024,1024]{1,0:T(8,128)(2,1)}, bf16[1024,1024]{1,0:T(8,128)(2,1)}) custom-call(f32[2048,768]{1,0:T(8,128)} %get-tuple-element.70.u.upre_c.refs_0_, f32[2048,128]{1,0:T(8,128)} %get-tuple-element.71.rec.refs_1_, f32[2048,512]{1,0:T(8,128)} %get-tuple-element.72.gate, ...), custom_call_target="tpu_custom_call" | custom-call | bytes 36900 | tf_op jit(solution)/shard_map/middle/pallas_call | solution.py:289
  88.0 1.7 collective-permute-start.12
  89.7 2.5 collective-permute-start.13
  92.6 4.9 %collective-permute-done.13.two = f32[8,2048]{1,0:T(8,128)S(1)} collective-permute-done((f32[8,2048]{1,0:T(8,128)}, f32[8,2048]{1,0:T(8,128)S(1)}, u32[]{:S(2)}, u32[]{:S(2)}) %collective-permute-start.13) | collective-permute-done | bytes 65568 | tf_op jit(solution)/shard_map/ppermute | solution.py:842
  100.8 4.4 collective-permute-start.16
  105.2 14.3 %turn.1 = (f32[2048,512]{1,0:T(8,128)}, bf16[2048,512]{1,0:T(8,128)(2,1)}, bf16[2048,512]{1,0:T(8,128)(2,1)}, f32[16,128,512]{2,1,0:T(8,128)}, f32[128,512]{1,0:...) custom-call(f32[2048,512]{1,0:T(8,128)} %get-tuple-element.82.scan, f32[2048,512]{1,0:T(8,128)} %get-tuple-element.72.gate, ...), custom_call_target="tpu_custom_call" | custom-call | bytes 36900 | tf_op jit(solution)/shard_map/turn/pallas_call | solution.py:383
  120.8 5.4 %convolution_bitcast_fusion.refs_11_.refs_2_.refs_5_.refs_6_ = f32[1024,512]{1,0:T(8,128)} fusion(bf16[2048,512]{1,0:T(8,128)(2,1)} %get-tuple-element.88, bf16[1,2048,1024]{2,1,0:T(8,128)(2,1)S(1)} %copy-done.1), kind=kOutput, calls=%fused_computation.4 | convolution fusion | flops 2147483648 | bytes 8388608 | tf_op jit(solution)/shard_map/dot_general | solution.py:1091
  126.2 2.6 collective-permute-start.15
  129.5 20.7 %back.2 = (f32[1024,768]{1,0:T(8,128)}, bf16[1024,128]{1,0:T(8,128)(2,1)}, f32[8,512]{1,0:T(8,128)}, f32[8,128]{1,0:T(8,128)}) custom-call(f32[2048,768]{1,0:T(8,128)} %get-tuple-element.70.u.upre_c.refs_0_, f32[2048,128]{1,0:T(8,128)} %get-tuple-element.71.rec.refs_1_, f32[2048,512]{1,0:T(8,128)} %get-tuple-element.84.refs_2_, ...), custom_call_target="tpu_custom_call" | custom-call | bytes 36900 | tf_op jit(solution)/shard_map/back/pallas_call | solution.py:545
  150.3 4.4 join.5.refs_11_.refs_2_
  154.7 2.0 collective-permute-start.18
  157.4 20.8 %back.3 = (f32[1024,768]{1,0:T(8,128)}, bf16[1024,128]{1,0:T(8,128)(2,1)}, f32[8,512]{1,0:T(8,128)}, f32[8,128]{1,0:T(8,128)}) custom-call(f32[2048,768]{1,0:T(8,128)} %get-tuple-element.70.u.upre_c.refs_0_, f32[2048,128]{1,0:T(8,128)} %get-tuple-element.71.rec.refs_1_, f32[2048,512]{1,0:T(8,128)} %get-tuple-element.84.refs_2_, ...), custom_call_target="tpu_custom_call" | custom-call | bytes 36900 | tf_op jit(solution)/shard_map/back/pallas_call | solution.py:545
  179.5 11.2 %rear.2 = (bf16[1024,1408]{1,0:T(8,128)(2,1)}, bf16[1024,1024]{1,0:T(8,128)(2,1)}, f32[8,768]{1,0:T(8,128)}) custom-call(f32[1024,768]{1,0:T(8,128)} %get-tuple-element.90.refs_0_, f32[2048,128]{1,0:T(8,128)} %get-tuple-element.71.rec.refs_1_, f32[2048,768]{1,0:T(8,128)} %get-tuple-element.91.refs_2_, bf16[2048,512]{1,0:T(8,128)(2,1)} %get-tuple-element.92.refs_3_, ...), custom_call_target="tpu_custom_call" | custom-call | bytes 36900 | tf_op jit(solution)/shard_map/rear/pallas_call | solution.py:635
  190.7 2.9 collective-permute-done.15.refs_1_
  194.2 7.4 %trade.2 = (bf16[1024,1024]{1,0:T(8,128)(2,1)}, bf16[1024,1024]{1,0:T(8,128)(2,1)}, bf16[1024,1024]{1,0:T(8,128)(2,1)}) custom-call(bf16[1024,1024]{1,0:T(8,128)(2,1)} %get-tuple-element.80.refs_0_, bf16[1024,1024]{1,0:T(8,128)(2,1)} %collective-permute-done.15.refs_1_, bf16[1024,1024]{1,0:T(8,128)(2,1)} %join.5.refs_11_.refs_2_, ...), custom_call_target="tpu_custom_call" | custom-call | bytes 36900 | tf_op jit(solution)/shard_map/trade/pallas_call | solution.py:787
  202.4 11.9 %collective-permute-start.22 = (bf16[1024,1024]{1,0:T(8,128)(2,1)}, bf16[1024,1024]{1,0:T(8,128)(2,1)S(1)}, u32[]{:S(2)}, u32[]{:S(2)}) collective-permute-start(bf16[1024,1024]{1,0:T(8,128)(2,1)} %get-tuple-element.108), channel_id=1, source_target_pairs={{0,1},{1,0},{2,3},{3,2},{4,5},{5,4},{6,7},{7,6},{8,9},{9,8},{10,11... | collective-permute-start | bytes 6291464 | tf_op jit(solution)/shard_map/ppermute | solution.py:824
  216.6 1.6 collective-permute-done.20.refs_5_
  218.8 11.3 %rear.3 = (bf16[1024,1408]{1,0:T(8,128)(2,1)}, bf16[1024,1024]{1,0:T(8,128)(2,1)}, f32[8,768]{1,0:T(8,128)}) custom-call(f32[1024,768]{1,0:T(8,128)} %get-tuple-element.94.refs_0_, f32[2048,128]{1,0:T(8,128)} %get-tuple-element.71.rec.refs_1_, f32[2048,768]{1,0:T(8,128)} %get-tuple-element.91.refs_2_, bf16[2048,512]{1,0:T(8,128)(2,1)} %get-tuple-element.92.refs_3_, ...), custom_call_target="tpu_custom_call" | custom-call | bytes 36900 | tf_op jit(solution)/shard_map/rear/pallas_call | solution.py:635
  230.1 9.5 %fusion.refs_1_.refs_2_.refs_3_.refs_4_ = f32[1024,1408]{1,0:T(8,128)S(1)} fusion(bf16[2048,1024]{1,0:T(8,128)(2,1)} %get-tuple-element.103, bf16[1024,1408]{1,0:T(8,128)(2,1)} %get-tuple-element.105, bf16[1024,1408]{1,0:T(8,128)(2,1)S(1)} %copy-done.39), kind=kOutput, calls=%fused_computation | convolution fusion | flops 5917114368 | bytes 15728640 | tf_op jit(solution)/shard_map/dot_general | solution.py:1157
  239.6 2.5 copy-done
  244.0 5.7 %trade.3 = (bf16[1024,1024]{1,0:T(8,128)(2,1)}, bf16[1024,1024]{1,0:T(8,128)(2,1)}) custom-call(bf16[1024,1024]{1,0:T(8,128)(2,1)} %get-tuple-element.99.refs_8_.refs_0_, bf16[1024,1024]{1,0:T(8,128)(2,1)} %copy-done.11, bf16[1024,1024]{1,0:T(8,128)(2,1)} %get-tuple-element.102.refs_2_.refs_0_, f32[8,128]{1,0:T(8,128)} %broadcast_in_dim.54.refs_5_.refs_3_.refs_4_.refs_6_, ...), custom_call_target="tpu_custom_call" | custom-call | bytes 36900 | tf_op jit(solution)/shard_map/trade/pallas_call | solution.py:787
  249.8 6.6 %collective-permute-done.22.refs_2_.refs_1_ = bf16[1024,1024]{1,0:T(8,128)(2,1)S(1)} collective-permute-done((bf16[1024,1024]{1,0:T(8,128)(2,1)}, bf16[1024,1024]{1,0:T(8,128)(2,1)S(1)}, u32[]{:S(2)}, u32[]{:S(2)}) %collective-permute-start.22) | collective-permute-done | bytes 2097184 | tf_op jit(solution)/shard_map/ppermute | solution.py:824
  257.7 5.2 %settle.2.refs_2_.refs_5_ = bf16[2048,1024]{1,0:T(8,128)(2,1)} custom-call(bf16[2048,1024]{1,0:T(8,128)(2,1)} %bitcast.70, f32[8,2048]{1,0:T(8,128)} %get-tuple-element.79.sums.refs_1_, bf16[1024,1024]{1,0:T(8,128)(2,1)} %copy-done.4, bf16[1024,1024]{1,0:T(8,128)(2,1)} %get-tuple-element.101.refs_9_.refs_3_, ...), custom_call_target="tpu_custom_call" | custom-call | bytes 36900 | tf_op jit(solution)/shard_map/settle/pallas_call | solution.py:700
  263.0 4.3 join.6.refs_0_.refs_2_.refs_3_
  267.3 2.0 collective-permute-start.23
  269.3 8.9 %collective-permute-start.21 = (bf16[1024,1024]{1,0:T(8,128)(2,1)}, bf16[1024,1024]{1,0:T(8,128)(2,1)S(1)}, u32[]{:S(2)}, u32[]{:S(2)}) collective-permute-start(bf16[1024,1024]{1,0:T(8,128)(2,1)} %get-tuple-element.106), channel_id=1, source_target_pairs={{0,1},{1,0},{2,3},{3,2},{4,5},{5,4},{6,7},{7,6},{8,9},{9,8},{10,11... | collective-permute-start | bytes 6291464 | tf_op jit(solution)/shard_map/ppermute | solution.py:824
  278.8 4.8 %other_core.1 = bf16[512,1920]{1,0:T(8,128)(2,1)} custom-call(s32[3]{0:T(128)} %pad_add_fusion.2.refs_0_, f32[1024,1408]{1,0:T(8,128)} %copy-done, f32[1024,512]{1,0:T(8,128)} %convolution_bitcast_fusion.refs_11_.refs_2_.refs_5_.refs_6_, bf16[1024,1024]{1,0:T(8,128)(2,1)} %join.6.refs_0_.refs_2_.refs_3_), custom_call_target="tpu_custom_call" | custom-call | bytes 36900 | tf_op jit(solution)/shard_map/other_core/pallas_call | solution.py:883
  283.6 4.3 join.7.refs_11_.refs_6_.refs_4_
  289.2 6.6 %split.1 = (f32[256,1024]{1,0:T(8,128)}, bf16[256,1024]{1,0:T(8,128)(2,1)}, f32[256,896]{1,0:T(8,128)}, bf16[256,896]{1,0:T(8,128)(2,1)}) custom-call(s32[3]{0:T(128)} %pad_add_fusion.2.refs_0_, f32[1024,1408]{1,0:T(8,128)} %copy-done, f32[1024,1408]{1,0:T(8,128)} %copy-done, f32[1024,1408]{1,0:T(8,128)} %copy-done, f32[1024,1408]{1,0:T(8,128)} %copy-done, ...), custom_call_target="tpu_custom_call" | custom-call | bytes 36900 | tf_op jit(solution)/shard_map/split/pallas_call | solution.py:883
  295.8 23.6 %collective-permute-done.21.refs_2_.refs_1_ = bf16[1024,1024]{1,0:T(8,128)(2,1)S(1)} collective-permute-done((bf16[1024,1024]{1,0:T(8,128)(2,1)}, bf16[1024,1024]{1,0:T(8,128)(2,1)S(1)}, u32[]{:S(2)}, u32[]{:S(2)}) %collective-permute-start.21) | collective-permute-done | bytes 2097184 | tf_op jit(solution)/shard_map/ppermute | solution.py:824
  320.7 5.3 %settle.3.refs_2_ = bf16[2048,1024]{1,0:T(8,128)(2,1)} custom-call(bf16[2048,1024]{1,0:T(8,128)(2,1)} %bitcast.71, f32[8,2048]{1,0:T(8,128)} %get-tuple-element.79.sums.refs_1_, bf16[1024,1024]{1,0:T(8,128)(2,1)} %copy-done.6, bf16[1024,1024]{1,0:T(8,128)(2,1)} %get-tuple-element.107.refs_6_.refs_3_, ...), custom_call_target="tpu_custom_call", output_to_operand_aliasing={{}: (5, {})} | custom-call | bytes 36900 | tf_op jit(solution)/shard_map/settle/pallas_call | solution.py:700
  326.0 4.5 join.8.refs_9_.refs_0_
  330.5 2.0 collective-permute-start.25
  339.7 5.4 %collective-permute-done.33 = f32[5120]{0:T(1024)S(1)} collective-permute-done((f32[5120]{0:T(1024)S(1)}, f32[5120]{0:T(1024)S(1)}, u32[]{:S(2)}, u32[]{:S(2)}) %collective-permute-start.33) | collective-permute-done | bytes 20512 | tf_op jit(solution)/shard_map/ppermute | solution.py:737
  347.0 3.6 second.1
  354.8 4.3 join.9.refs_7_.refs_4_
  360.4 27.6 %collective-permute-done.29.refs_3_ = bf16[1024,1024]{1,0:T(8,128)(2,1)} collective-permute-done((bf16[1024,1024]{1,0:T(8,128)(2,1)S(1)}, bf16[1024,1024]{1,0:T(8,128)(2,1)}, u32[]{:S(2)}, u32[]{:S(2)}) %collective-permute-start.29) | collective-permute-done | bytes 2097184 | tf_op jit(solution)/shard_map/ppermute | solution.py:816
  388.0 6.6 %finish.2 = (f32[2048,1024]{1,0:T(8,128)}, f32[128,1024]{1,0:T(8,128)}, f32[128,896]{1,0:T(8,128)}) custom-call(bf16[2048,1024]{1,0:T(8,128)(2,1)} %bitcast.72, bf16[2048,1024]{1,0:T(8,128)(2,1)} %bitcast.76, f32[8,1024]{1,0:T(8,128)} %get-tuple-element.110.refs_2_, ...), custom_call_target="tpu_custom_call", output_to_operand_aliasing={{1}: (8, {}), {2}: (9, {})} | custom-call | bytes 36900 | tf_op jit(solution)/shard_map/finish/pallas_call | solution.py:700
  397.1 7.7 %collective-permute-start.35 = (f32[34176]{0:T(1024)S(1)}, f32[34176]{0:T(1024)S(1)}, u32[]{:S(2)}, u32[]{:S(2)}) collective-permute-start(f32[34176]{0:T(1024)S(1)} %pad_maximum_fusion.1), channel_id=1, source_target_pairs={{0,1},{1,0},{2,3},{3,2},{4,5},{5,4},{6,7},{7,6},{8,9},{9,8},{10,11... | collective-permute-start | bytes 410120 | tf_op jit(solution)/shard_map/ppermute | solution.py:737
  406.6 31.7 %collective-permute-done.35 = f32[34176]{0:T(1024)S(1)} collective-permute-done((f32[34176]{0:T(1024)S(1)}, f32[34176]{0:T(1024)S(1)}, u32[]{:S(2)}, u32[]{:S(2)}) %collective-permute-start.35) | collective-permute-done | bytes 136736 | tf_op jit(solution)/shard_map/ppermute | solution.py:737
  439.9 4.9 %collective-permute-done.36 = f32[34176]{0:T(1024)S(1)} collective-permute-done((f32[34176]{0:T(1024)S(1)}, f32[34176]{0:T(1024)S(1)}, u32[]{:S(2)}, u32[]{:S(2)}) %collective-permute-start.36) | collective-permute-done | bytes 136736 | tf_op jit(solution)/shard_map/ppermute | solution.py:737
  447.1 6.6 %finish.3 = f32[2048,1024]{1,0:T(8,128)} custom-call(bf16[2048,1024]{1,0:T(8,128)(2,1)} %bitcast.73, bf16[2048,1024]{1,0:T(8,128)(2,1)} %bitcast.77, f32[8,1024]{1,0:T(8,128)} %get-tuple-element.110.refs_2_, bf16[1024,1024]{1,0:T(8,128)(2,1)} %collective-permute-done.28.refs_3_, ...), custom_call_target="tpu_custom_call", output_to_operand_aliasing={{}: (6, {})} | custom-call | bytes 36900 | tf_op jit(solution)/shard_map/finish/pallas_call | solution.py:700
  (220 shorter events, 64.9 us)
Async XLA Ops:
  7.2 27.3 %copy-start.20 = (s32[1,2048]{1,0:T(1,128)S(1)}, s32[1,2048]{1,0:T(1,128)}, u32[]{:S(2)}) copy-start(s32[1,2048]{1,0:T(1,128)} %param.17) | copy-start | bytes 24580
  7.2 25.8 %copy-start.36 = (f32[2,128]{1,0:T(2,128)S(1)}, f32[2,128]{1,0:T(2,128)}, u32[]{:S(2)}) copy-start(f32[2,128]{1,0:T(2,128)} %param.26) | copy-start | bytes 3076
  7.2 25.8 %copy-start.34 = (f32[512]{0:T(512)S(1)}, f32[512]{0:T(512)}, u32[]{:S(2)}) copy-start(f32[512]{0:T(512)} %param.24) | copy-start | bytes 6148
  7.2 25.8 %copy-start.33 = (f32[4,2,128]{2,1,0:T(2,128)S(1)}, f32[4,2,128]{2,1,0:T(2,128)}, u32[]{:S(2)}) copy-start(f32[4,2,128]{2,1,0:T(2,128)} %param.25) | copy-start | bytes 12292
  7.2 26.6 %copy-start.32 = (f32[4,512]{1,0:T(4,128)S(1)}, f32[4,512]{1,0:T(4,128)}, u32[]{:S(2)}) copy-start(f32[4,512]{1,0:T(4,128)} %param.23) | copy-start | bytes 24580
  7.2 61.7 %all-gather.2.cloned.1.call-start = ((), (), s32[]{:S(2)}) async-start(), calls=%async_computation | async-start | bytes 1179648 | tf_op jit(solution)/shard_map/all_gather | solution.py:1047
  10.9 28.1 %copy-start.7 = (bf16[128,1408]{1,0:T(8,128)(2,1)}, bf16[128,1408]{1,0:T(8,128)(2,1)S(1)}, u32[]{:S(2)}) copy-start(bf16[128,1408]{1,0:T(8,128)(2,1)S(1)} %concatenate.56.refs_0_) | copy-start | bytes 1081348
  10.9 13.2 %collective-permute-start.2 = (bf16[128,1408]{1,0:T(8,128)(2,1)S(1)}, bf16[128,1408]{1,0:T(8,128)(2,1)S(1)}, u32[]{:S(2)}, u32[]{:S(2)}) collective-permute-start(bf16[128,1408]{1,0:T(8,128)(2,1)S(1)} %concatenate.56.refs_0_), channel_id=1, source_target_pairs={{0,8},{8,0},{16,24},{24,16},{1,9},{9,1},{17,25},{25,17},{2,10},{10... | collective-permute-start | bytes 1081352 | tf_op jit(solution)/shard_map/ppermute | solution.py:988
  13.9 10.7 %collective-permute-start.3 = (bf16[128,1408]{1,0:T(8,128)(2,1)S(1)}, bf16[128,1408]{1,0:T(8,128)(2,1)S(1)}, u32[]{:S(2)}, u32[]{:S(2)}) collective-permute-start(bf16[128,1408]{1,0:T(8,128)(2,1)S(1)} %concatenate.56.refs_0_), channel_id=1, source_target_pairs={{0,16},{8,24},{16,0},{24,8},{1,17},{9,25},{17,1},{25,9},{2,18},{10... | collective-permute-start | bytes 1081352 | tf_op jit(solution)/shard_map/ppermute | solution.py:988
  15.4 23.5 %collective-permute-start.6 = (bf16[128,1408]{1,0:T(8,128)(2,1)S(1)}, bf16[128,1408]{1,0:T(8,128)(2,1)S(1)}, u32[]{:S(2)}, u32[]{:S(2)}) collective-permute-start(bf16[128,1408]{1,0:T(8,128)(2,1)S(1)} %concatenate.56.refs_0_), channel_id=1, source_target_pairs={{0,4},{4,0},{1,5},{5,1},{2,6},{6,2},{3,7},{7,3},{8,12},{12,8},{9,1... | collective-permute-start | bytes 1081352 | tf_op jit(solution)/shard_map/ppermute | solution.py:988
  16.1 18.3 %collective-permute-start.1 = (s32[3]{0:T(128)S(1)}, s32[3]{0:T(128)S(1)}, u32[]{:S(2)}, u32[]{:S(2)}) collective-permute-start(s32[3]{0:T(128)S(1)} %slice_bitcast_fusion.5), channel_id=1, source_target_pairs={{0,4},{1,5},{2,6},{3,7},{8,12},{9,13},{10,14},{11,15},{16,20},{17,... | collective-permute-start | bytes 44 | tf_op jit(solution)/shard_map/ppermute | solution.py:722
  19.3 17.3 %collective-permute-start = (bf16[16,1024]{1,0:T(8,128)(2,1)S(1)}, bf16[16,1024]{1,0:T(8,128)(2,1)S(1)}, u32[]{:S(2)}, u32[]{:S(2)}) collective-permute-start(bf16[16,1024]{1,0:T(8,128)(2,1)S(1)} %slice_bitcast_fusion.2), channel_id=1, source_target_pairs={{0,4},{1,5},{2,6},{3,7},{8,12},{9,13},{10,14},{11,15},{16,20},{17,... | collective-permute-start | bytes 98312 | tf_op jit(solution)/shard_map/ppermute | solution.py:722
  24.0 5.9 %collective-permute-start.5 = (bf16[64,1408]{1,0:T(8,128)(2,1)S(1)}, bf16[64,1408]{1,0:T(8,128)(2,1)S(1)}, u32[]{:S(2)}, u32[]{:S(2)}) collective-permute-start(bf16[64,1408]{1,0:T(8,128)(2,1)S(1)} %slice.204), channel_id=1, source_target_pairs={{0,16},{8,24},{16,0},{24,8},{1,17},{9,25},{17,1},{25,9},{2,18},{10... | collective-permute-start | bytes 540680 | tf_op jit(solution)/shard_map/ppermute | solution.py:988
  24.6 5.6 %collective-permute-start.4 = (bf16[64,1408]{1,0:T(8,128)(2,1)S(1)}, bf16[64,1408]{1,0:T(8,128)(2,1)S(1)}, u32[]{:S(2)}, u32[]{:S(2)}) collective-permute-start(bf16[64,1408]{1,0:T(8,128)(2,1)S(1)} %slice.203), channel_id=1, source_target_pairs={{0,8},{8,0},{16,24},{24,16},{1,9},{9,1},{17,25},{25,17},{2,10},{10... | collective-permute-start | bytes 540680 | tf_op jit(solution)/shard_map/ppermute | solution.py:988
  35.8 3.2 collective-permute-start.7
  35.8 3.2 collective-permute-start.8
  36.5 2.4 collective-permute-start.10
  36.6 2.3 collective-permute-start.9
  39.9 27.7 %copy-start.38 = (f32[8]{0:T(128)S(1)}, f32[8]{0:T(128)}, u32[]{:S(2)}) copy-start(f32[8]{0:T(128)} %param.29) | copy-start | bytes 100
  39.9 27.8 %copy-start.35 = (f32[512]{0:T(512)S(1)}, f32[512]{0:T(512)}, u32[]{:S(2)}) copy-start(f32[512]{0:T(512)} %param.30) | copy-start | bytes 6148
  65.6 3.3 collective-permute-start.11
  88.0 4.6 %collective-permute-start.12 = (f32[8,2048]{1,0:T(8,128)}, f32[8,2048]{1,0:T(8,128)S(1)}, u32[]{:S(2)}, u32[]{:S(2)}) collective-permute-start(f32[8,2048]{1,0:T(8,128)} %get-tuple-element.76.own), channel_id=1, source_target_pairs={{0,1},{1,0},{2,3},{3,2},{4,5},{5,4},{6,7},{7,6},{8,9},{9,8},{10,11... | collective-permute-start | bytes 196616 | tf_op jit(solution)/shard_map/ppermute | solution.py:842
  89.7 7.9 %collective-permute-start.13 = (f32[8,2048]{1,0:T(8,128)}, f32[8,2048]{1,0:T(8,128)S(1)}, u32[]{:S(2)}, u32[]{:S(2)}) collective-permute-start(f32[8,2048]{1,0:T(8,128)} %get-tuple-element.76.own), channel_id=1, source_target_pairs={{0,2},{1,3},{2,0},{3,1},{4,6},{5,7},{6,4},{7,5},{8,10},{9,11},{10,... | collective-permute-start | bytes 196616 | tf_op jit(solution)/shard_map/ppermute | solution.py:842
  92.2 6.4 %collective-permute-start.14 = (f32[8,2048]{1,0:T(8,128)}, f32[8,2048]{1,0:T(8,128)S(1)}, u32[]{:S(2)}, u32[]{:S(2)}) collective-permute-start(f32[8,2048]{1,0:T(8,128)} %get-tuple-element.76.own), channel_id=1, source_target_pairs={{0,3},{1,2},{2,1},{3,0},{4,7},{5,6},{6,5},{7,4},{8,11},{9,10},{10,... | collective-permute-start | bytes 196616 | tf_op jit(solution)/shard_map/ppermute | solution.py:842
  100.8 49.5 %collective-permute-start.16 = (bf16[1024,1024]{1,0:T(8,128)(2,1)}, bf16[1024,1024]{1,0:T(8,128)(2,1)}, u32[]{:S(2)}, u32[]{:S(2)}) collective-permute-start(bf16[1024,1024]{1,0:T(8,128)(2,1)} %get-tuple-element.81.refs_0_), channel_id=1, source_target_pairs={{0,1},{3,2},{4,5},{7,6},{8,9},{11,10},{12,13},{15,14},{16,17},{19,... | collective-permute-start | bytes 6291464 | tf_op jit(solution)/shard_map/ppermute | solution.py:804
  105.2 15.6 %copy-start.1 = (bf16[1,2048,1024]{2,1,0:T(8,128)(2,1)S(1)}, bf16[1,2048,1024]{2,1,0:T(8,128)(2,1)}, u32[]{:S(2)}) copy-start(bf16[1,2048,1024]{2,1,0:T(8,128)(2,1)} %param.18) | copy-start | bytes 12582916
  119.5 9.3 %collective-permute-start.17 = (f32[128,512]{1,0:T(8,128)}, f32[128,512]{1,0:T(8,128)S(1)}, u32[]{:S(2)}, u32[]{:S(2)}) collective-permute-start(f32[128,512]{1,0:T(8,128)} %get-tuple-element.87), channel_id=1, source_target_pairs={{4,0},{5,1},{6,2},{7,3},{12,8},{13,9},{14,10},{15,11},{20,16},{21,... | collective-permute-start | bytes 786440 | tf_op jit(solution)/shard_map/ppermute | solution.py:722
  126.2 67.4 %collective-permute-start.15 = (bf16[1024,1024]{1,0:T(8,128)(2,1)S(1)}, bf16[1024,1024]{1,0:T(8,128)(2,1)}, u32[]{:S(2)}, u32[]{:S(2)}) collective-permute-start(bf16[1024,1024]{1,0:T(8,128)(2,1)S(1)} %copy-done.5), channel_id=1, source_target_pairs={{0,1},{3,2},{4,5},{7,6},{8,9},{11,10},{12,13},{15,14},{16,17},{19,... | collective-permute-start | bytes 6291464 | tf_op jit(solution)/shard_map/ppermute | solution.py:804
  154.7 38.9 %collective-permute-start.18 = (bf16[1024,1024]{1,0:T(8,128)(2,1)}, bf16[1024,1024]{1,0:T(8,128)(2,1)}, u32[]{:S(2)}, u32[]{:S(2)}) collective-permute-start(bf16[1024,1024]{1,0:T(8,128)(2,1)} %join.5.refs_11_.refs_2_), channel_id=1, source_target_pairs={{1,2},{2,1},{5,6},{6,5},{9,10},{10,9},{13,14},{14,13},{17,18},{18,... | collective-permute-start | bytes 6291464 | tf_op jit(solution)/shard_map/ppermute | solution.py:813
  201.6 41.1 %collective-permute-start.19 = (bf16[1024,1024]{1,0:T(8,128)(2,1)}, bf16[1024,1024]{1,0:T(8,128)(2,1)S(1)}, u32[]{:S(2)}, u32[]{:S(2)}) collective-permute-start(bf16[1024,1024]{1,0:T(8,128)(2,1)} %get-tuple-element.99.refs_8_.refs_0_), channel_id=1, source_target_pairs={{1,2},{2,1},{5,6},{6,5},{9,10},{10,9},{13,14},{14,13},{17,18},{18,... | collective-permute-start | bytes 6291464 | tf_op jit(solution)/shard_map/ppermute | solution.py:813
  202.4 54.0 %collective-permute-start.22 = (bf16[1024,1024]{1,0:T(8,128)(2,1)}, bf16[1024,1024]{1,0:T(8,128)(2,1)S(1)}, u32[]{:S(2)}, u32[]{:S(2)}) collective-permute-start(bf16[1024,1024]{1,0:T(8,128)(2,1)} %get-tuple-element.108), channel_id=1, source_target_pairs={{0,1},{1,0},{2,3},{3,2},{4,5},{5,4},{6,7},{7,6},{8,9},{9,8},{10,11... | collective-permute-start | bytes 6291464 | tf_op jit(solution)/shard_map/ppermute | solution.py:824
  215.1 3.1 collective-permute-start.20
  267.3 16.3 %collective-permute-start.23 = (bf16[1024,1024]{1,0:T(8,128)(2,1)}, bf16[1024,1024]{1,0:T(8,128)(2,1)}, u32[]{:S(2)}, u32[]{:S(2)}) collective-permute-start(bf16[1024,1024]{1,0:T(8,128)(2,1)} %join.6.refs_0_.refs_2_.refs_3_), channel_id=1, source_target_pairs={{1,2},{2,1},{5,6},{6,5},{9,10},{10,9},{13,14},{14,13},{17,18},{18,... | collective-permute-start | bytes 6291464 | tf_op jit(solution)/shard_map/ppermute | solution.py:813
  269.3 50.1 %collective-permute-start.21 = (bf16[1024,1024]{1,0:T(8,128)(2,1)}, bf16[1024,1024]{1,0:T(8,128)(2,1)S(1)}, u32[]{:S(2)}, u32[]{:S(2)}) collective-permute-start(bf16[1024,1024]{1,0:T(8,128)(2,1)} %get-tuple-element.106), channel_id=1, source_target_pairs={{0,1},{1,0},{2,3},{3,2},{4,5},{5,4},{6,7},{7,6},{8,9},{9,8},{10,11... | collective-permute-start | bytes 6291464 | tf_op jit(solution)/shard_map/ppermute | solution.py:824
  283.6 4.3 collective-permute-start.24
  330.5 24.3 %collective-permute-start.25 = (bf16[1024,1024]{1,0:T(8,128)(2,1)}, bf16[1024,1024]{1,0:T(8,128)(2,1)}, u32[]{:S(2)}, u32[]{:S(2)}) collective-permute-start(bf16[1024,1024]{1,0:T(8,128)(2,1)} %join.8.refs_9_.refs_0_), channel_id=1, source_target_pairs={{1,2},{2,1},{5,6},{6,5},{9,10},{10,9},{13,14},{14,13},{17,18},{18,... | collective-permute-start | bytes 6291464 | tf_op jit(solution)/shard_map/ppermute | solution.py:813
  332.5 55.5 %collective-permute-start.29 = (bf16[1024,1024]{1,0:T(8,128)(2,1)S(1)}, bf16[1024,1024]{1,0:T(8,128)(2,1)}, u32[]{:S(2)}, u32[]{:S(2)}) collective-permute-start(bf16[1024,1024]{1,0:T(8,128)(2,1)S(1)} %copy-done.2), channel_id=1, source_target_pairs={{1,0},{2,3},{5,4},{6,7},{9,8},{10,11},{13,12},{14,15},{17,16},{18,... | collective-permute-start | bytes 6291464 | tf_op jit(solution)/shard_map/ppermute | solution.py:816
  335.2 10.9 %collective-permute-start.26 = (bf16[256,1024]{1,0:T(8,128)(2,1)}, bf16[256,1024]{1,0:T(8,128)(2,1)S(1)}, u32[]{:S(2)}, u32[]{:S(2)}) collective-permute-start(bf16[256,1024]{1,0:T(8,128)(2,1)} %get-tuple-element.109.refs_7_), channel_id=1, source_target_pairs={{0,8},{8,0},{16,24},{24,16},{1,9},{9,1},{17,25},{25,17},{2,10},{10... | collective-permute-start | bytes 1572872 | tf_op jit(solution)/shard_map/ppermute | solution.py:918
  335.9 10.2 %collective-permute-start.27 = (bf16[256,896]{1,0:T(8,128)(2,1)}, bf16[256,896]{1,0:T(8,128)(2,1)S(1)}, u32[]{:S(2)}, u32[]{:S(2)}) collective-permute-start(bf16[256,896]{1,0:T(8,128)(2,1)} %get-tuple-element.113), channel_id=1, source_target_pairs={{0,16},{8,24},{16,0},{24,8},{1,17},{9,25},{17,1},{25,9},{2,18},{10... | collective-permute-start | bytes 1376264 | tf_op jit(solution)/shard_map/ppermute | solution.py:918
  336.9 1.3 collective-permute-start.32
  338.2 6.9 %collective-permute-start.33 = (f32[5120]{0:T(1024)S(1)}, f32[5120]{0:T(1024)S(1)}, u32[]{:S(2)}, u32[]{:S(2)}) collective-permute-start(f32[5120]{0:T(1024)S(1)} %fusion.22), channel_id=1, source_target_pairs={{0,8},{8,0},{16,24},{24,16},{1,9},{9,1},{17,25},{25,17},{2,10},{10... | collective-permute-start | bytes 61448 | tf_op jit(solution)/shard_map/ppermute | solution.py:737
  345.1 6.2 %collective-permute-start.34 = (f32[5120]{0:T(1024)S(1)}, f32[5120]{0:T(1024)S(1)}, u32[]{:S(2)}, u32[]{:S(2)}) collective-permute-start(f32[5120]{0:T(1024)S(1)} %add.90), channel_id=1, source_target_pairs={{0,16},{8,24},{16,0},{24,8},{1,17},{9,25},{17,1},{25,9},{2,18},{10... | collective-permute-start | bytes 61448 | tf_op jit(solution)/shard_map/ppermute | solution.py:737
  350.6 43.9 %collective-permute-start.30 = (bf16[128,896]{1,0:T(8,128)(2,1)}, bf16[128,896]{1,0:T(8,128)(2,1)S(1)}, u32[]{:S(2)}, u32[]{:S(2)}) collective-permute-start(bf16[128,896]{1,0:T(8,128)(2,1)} %get-tuple-element.119), channel_id=1, source_target_pairs={{0,8},{8,0},{16,24},{24,16},{1,9},{9,1},{17,25},{25,17},{2,10},{10... | collective-permute-start | bytes 688136 | tf_op jit(solution)/shard_map/ppermute | solution.py:918
  353.7 42.0 %collective-permute-start.31 = (bf16[128,1024]{1,0:T(8,128)(2,1)}, bf16[128,1024]{1,0:T(8,128)(2,1)S(1)}, u32[]{:S(2)}, u32[]{:S(2)}) collective-permute-start(bf16[128,1024]{1,0:T(8,128)(2,1)} %get-tuple-element.114.refs_2_), channel_id=1, source_target_pairs={{0,16},{8,24},{16,0},{24,8},{1,17},{9,25},{17,1},{25,9},{2,18},{10... | collective-permute-start | bytes 786440 | tf_op jit(solution)/shard_map/ppermute | solution.py:918
  359.1 88.0 %collective-permute-start.28 = (bf16[1024,1024]{1,0:T(8,128)(2,1)}, bf16[1024,1024]{1,0:T(8,128)(2,1)}, u32[]{:S(2)}, u32[]{:S(2)}) collective-permute-start(bf16[1024,1024]{1,0:T(8,128)(2,1)} %join.9.refs_7_.refs_4_), channel_id=1, source_target_pairs={{1,0},{2,3},{5,4},{6,7},{9,8},{10,11},{13,12},{14,15},{17,16},{18,... | collective-permute-start | bytes 6291464 | tf_op jit(solution)/shard_map/ppermute | solution.py:816
  396.8 49.8 %copy-start.37 = (bf16[128]{0:T(256)(128)(2,1)S(1)}, bf16[128]{0:T(256)(128)(2,1)}, u32[]{:S(2)}) copy-start(bf16[128]{0:T(256)(128)(2,1)} %param.19) | copy-start | bytes 772
  397.1 41.2 %collective-permute-start.35 = (f32[34176]{0:T(1024)S(1)}, f32[34176]{0:T(1024)S(1)}, u32[]{:S(2)}, u32[]{:S(2)}) collective-permute-start(f32[34176]{0:T(1024)S(1)} %pad_maximum_fusion.1), channel_id=1, source_target_pairs={{0,1},{1,0},{2,3},{3,2},{4,5},{5,4},{6,7},{7,6},{8,9},{9,8},{10,11... | collective-permute-start | bytes 410120 | tf_op jit(solution)/shard_map/ppermute | solution.py:737
  438.3 6.5 %collective-permute-start.36 = (f32[34176]{0:T(1024)S(1)}, f32[34176]{0:T(1024)S(1)}, u32[]{:S(2)}, u32[]{:S(2)}) collective-permute-start(f32[34176]{0:T(1024)S(1)} %fusion.21), channel_id=1, source_target_pairs={{0,2},{1,3},{2,0},{3,1},{4,6},{5,7},{6,4},{7,5},{8,10},{9,11},{10,... | collective-permute-start | bytes 410120 | tf_op jit(solution)/shard_map/ppermute | solution.py:737
  (30 other events, 119.7 us)
Sparse Core Ops, SparseCore 0:
  33.1 23.4 all-gather.1

commit v2 on v1

--- a/solution.py
+++ b/solution.py
@@ -1161,14 +1161,14 @@
         [sum_b], rears[1][1], outer, (w_grad[:8, :LANES],)
     )
     sum_c, sum_d = d_normed
+    done = advance([sum_c], done)
     block_out = settle(0, None, done)
+    owners.send((block_out,))
     done = advance([sum_c], (block_out,))
-    owners.send(done)
-    done = advance([sum_c], done)
     sent = owners.send(done)
-    block_out = settle(1, block_out, done + (sent,))
-    done = advance([sum_d], (block_out,))
-    sent, kept = owners.send(done)
+    done = advance([sum_d], done + (sent,))
+    block_out = settle(1, block_out, done)
+    sent, kept = owners.send((block_out,))
     done = advance([sum_d], (sent,))
     hidden_grad, kept = finish(0, None, done, kept)
     both_owned = owners.send(kept)

time: 463 us -> 453 us (0.978)
  waiting for transfers between devices: 116 us -> 105 us
    ppermute x2, waiting for transfers between devices: 30.3 us -> 24.4 us  [advance_and_begin(): come = lax.ppermute(both, 'tp', [(0, 1), (1, 0), (2, 3), (3, 2)])]
    ppermute x2, waiting for transfers between devices: 27.6 us -> 22.7 us  [joined(): self.given = lax.ppermute(value, 'tp', [(1, 0), (2, 3)])]
    unnamed x90 -> x88, local copies, waits for them, and re-layouts: 17.7 us -> 17.7 us
  transfers between devices with their start and end apart: 38 -> 38, of which waited for: 15 -> 15; matrix products, arithmetic and copies ran while one was open for 9% -> 10% of each run, Pallas kernels for 32% -> 35%
where the time goes in v2:
time: 453 us; the launch traced here: 451 us
  Pallas kernels  199 us (44%)
  waiting for transfers between devices  105 us (23%)
  starting transfers between devices  71.1 us (16%)
  local copies, waits for them, and re-layouts  35.7 us (8%)
  matrix products  15.7 us (3%)
  between operations  14.7 us (3%)
  other arithmetic  9.04 us (2%)
    ppermute x5, waiting for transfers between devices, butterfly_sum(): value = value + lax.ppermute(value, axis, pairs)  43.2 us
    pallas_call x2, Pallas kernels, back(): pl.pallas_call(ordered(back_kernel, 11, len(after)), grid=(steps,), in_sp...  41.5 us
    pallas_call x1, Pallas kernels, front(): pl.pallas_call(functools.partial(front_kernel, gain_lane), grid=(steps,),...  25.6 us
    ppermute x2, waiting for transfers between devices, advance_and_begin(): come = lax.ppermute(both, 'tp', [(0, 1), (1, 0), (2, 3), (3, 2)])  24.4 us
    pallas_call x4, Pallas kernels, by_group(): pl.pallas_call(ordered(kernel, count, len(after) + len(held)), grid=(step...  23.6 us
    ppermute x2, waiting for transfers between devices, joined(): self.given = lax.ppermute(value, 'tp', [(1, 0), (2, 3)])  22.7 us
    pallas_call x2, Pallas kernels, rear(): pl.pallas_call(ordered(rear_kernel, 8, len(after)), grid=(steps,), in_spe...  22.4 us
    pallas_call x5, Pallas kernels, join(): pl.pallas_call(ordered(functools.partial(join_kernel, len(pairs)), 2 * le...  21.8 us
  transfers between devices with their start and end apart: 38, of which 15 were waited for; matrix products, arithmetic and copies ran while one was open for 10% of the time, Pallas kernels for 35%

profile of v2, /device:TPU:0, one launch (start us, length us, event | category | flops | bytes accessed | tf_op | source)
XLA Modules:
  0.0 450.5 jit_solution(11935247276906393580)
XLA Ops:
  10.9 3.0 collective-permute-start.2
  16.1 2.4 collective-permute-start.1
  26.4 3.6 collective-permute-done.5.refs_4_.refs_2_
  31.3 1.7 flip.1
  39.9 25.6 %front.1 = (bf16[2048,1024]{1,0:T(8,128)(2,1)}, f32[2048,512]{1,0:T(8,128)}, f32[2048,768]{1,0:T(8,128)}, f32[2048,768]{1,0:T(8,128)}, f32[2048,128]{1,0:T(8,128...) custom-call(s32[10]{0:T(128)} %stack.79.starts, ...), custom_call_target="tpu_custom_call" | custom-call | bytes 36900 | tf_op jit(solution)/shard_map/front/pallas_call | solution.py:170
  65.5 2.1 collective-permute-start.11
  69.6 18.4 %middle.1 = (f32[2048,512]{1,0:T(8,128)}, f32[2048,512]{1,0:T(8,128)}, f32[8,2048]{1,0:T(8,128)}, bf16[1024,1024]{1,0:T(8,128)(2,1)}, bf16[1024,1024]{1,0:T(8,128)(2,1)}) custom-call(f32[2048,768]{1,0:T(8,128)} %get-tuple-element.70.u.upre_c.refs_0_, f32[2048,128]{1,0:T(8,128)} %get-tuple-element.71.rec.refs_1_, f32[2048,512]{1,0:T(8,128)} %get-tuple-element.72.gate, ...), custom_call_target="tpu_custom_call" | custom-call | bytes 36900 | tf_op jit(solution)/shard_map/middle/pallas_call | solution.py:289
  88.1 1.7 collective-permute-start.12
  89.7 2.6 collective-permute-start.13
  92.7 4.9 %collective-permute-done.13.two = f32[8,2048]{1,0:T(8,128)S(1)} collective-permute-done((f32[8,2048]{1,0:T(8,128)}, f32[8,2048]{1,0:T(8,128)S(1)}, u32[]{:S(2)}, u32[]{:S(2)}) %collective-permute-start.13) | collective-permute-done | bytes 65568 | tf_op jit(solution)/shard_map/ppermute | solution.py:842
  100.8 4.4 collective-permute-start.16
  105.2 14.3 %turn.1 = (f32[2048,512]{1,0:T(8,128)}, bf16[2048,512]{1,0:T(8,128)(2,1)}, bf16[2048,512]{1,0:T(8,128)(2,1)}, f32[16,128,512]{2,1,0:T(8,128)}, f32[128,512]{1,0:...) custom-call(f32[2048,512]{1,0:T(8,128)} %get-tuple-element.82.scan, f32[2048,512]{1,0:T(8,128)} %get-tuple-element.72.gate, ...), custom_call_target="tpu_custom_call" | custom-call | bytes 36900 | tf_op jit(solution)/shard_map/turn/pallas_call | solution.py:383
  120.8 5.4 %convolution_bitcast_fusion.refs_11_.refs_2_.refs_5_.refs_6_ = f32[1024,512]{1,0:T(8,128)} fusion(bf16[2048,512]{1,0:T(8,128)(2,1)} %get-tuple-element.88, bf16[1,2048,1024]{2,1,0:T(8,128)(2,1)S(1)} %copy-done.1), kind=kOutput, calls=%fused_computation.4 | convolution fusion | flops 2147483648 | bytes 8388608 | tf_op jit(solution)/shard_map/dot_general | solution.py:1091
  126.2 2.6 collective-permute-start.15
  129.5 20.7 %back.2 = (f32[1024,768]{1,0:T(8,128)}, bf16[1024,128]{1,0:T(8,128)(2,1)}, f32[8,512]{1,0:T(8,128)}, f32[8,128]{1,0:T(8,128)}) custom-call(f32[2048,768]{1,0:T(8,128)} %get-tuple-element.70.u.upre_c.refs_0_, f32[2048,128]{1,0:T(8,128)} %get-tuple-element.71.rec.refs_1_, f32[2048,512]{1,0:T(8,128)} %get-tuple-element.84.refs_2_, ...), custom_call_target="tpu_custom_call" | custom-call | bytes 36900 | tf_op jit(solution)/shard_map/back/pallas_call | solution.py:545
  150.3 4.4 join.5.refs_11_.refs_2_
  154.7 2.0 collective-permute-start.18
  157.4 20.8 %back.3 = (f32[1024,768]{1,0:T(8,128)}, bf16[1024,128]{1,0:T(8,128)(2,1)}, f32[8,512]{1,0:T(8,128)}, f32[8,128]{1,0:T(8,128)}) custom-call(f32[2048,768]{1,0:T(8,128)} %get-tuple-element.70.u.upre_c.refs_0_, f32[2048,128]{1,0:T(8,128)} %get-tuple-element.71.rec.refs_1_, f32[2048,512]{1,0:T(8,128)} %get-tuple-element.84.refs_2_, ...), custom_call_target="tpu_custom_call" | custom-call | bytes 36900 | tf_op jit(solution)/shard_map/back/pallas_call | solution.py:545
  179.5 11.2 %rear.2 = (bf16[1024,1408]{1,0:T(8,128)(2,1)}, bf16[1024,1024]{1,0:T(8,128)(2,1)}, f32[8,768]{1,0:T(8,128)}) custom-call(f32[1024,768]{1,0:T(8,128)} %get-tuple-element.90.refs_0_, f32[2048,128]{1,0:T(8,128)} %get-tuple-element.71.rec.refs_1_, f32[2048,768]{1,0:T(8,128)} %get-tuple-element.91.refs_2_, bf16[2048,512]{1,0:T(8,128)(2,1)} %get-tuple-element.92.refs_3_, ...), custom_call_target="tpu_custom_call" | custom-call | bytes 36900 | tf_op jit(solution)/shard_map/rear/pallas_call | solution.py:635
  190.7 3.0 collective-permute-done.15.refs_1_
  194.2 7.5 %trade.2 = (bf16[1024,1024]{1,0:T(8,128)(2,1)}, bf16[1024,1024]{1,0:T(8,128)(2,1)}, bf16[1024,1024]{1,0:T(8,128)(2,1)}) custom-call(bf16[1024,1024]{1,0:T(8,128)(2,1)} %get-tuple-element.80.refs_0_, bf16[1024,1024]{1,0:T(8,128)(2,1)} %collective-permute-done.15.refs_1_, bf16[1024,1024]{1,0:T(8,128)(2,1)} %join.5.refs_11_.refs_2_, ...), custom_call_target="tpu_custom_call" | custom-call | bytes 36900 | tf_op jit(solution)/shard_map/trade/pallas_call | solution.py:787
  202.5 11.9 %collective-permute-start.22 = (bf16[1024,1024]{1,0:T(8,128)(2,1)}, bf16[1024,1024]{1,0:T(8,128)(2,1)S(1)}, u32[]{:S(2)}, u32[]{:S(2)}) collective-permute-start(bf16[1024,1024]{1,0:T(8,128)(2,1)} %get-tuple-element.108), channel_id=1, source_target_pairs={{0,1},{1,0},{2,3},{3,2},{4,5},{5,4},{6,7},{7,6},{8,9},{9,8},{10,11... | collective-permute-start | bytes 6291464 | tf_op jit(solution)/shard_map/ppermute | solution.py:824
  216.7 1.6 collective-permute-done.20.refs_5_
  218.9 11.2 %rear.3 = (bf16[1024,1408]{1,0:T(8,128)(2,1)}, bf16[1024,1024]{1,0:T(8,128)(2,1)}, f32[8,768]{1,0:T(8,128)}) custom-call(f32[1024,768]{1,0:T(8,128)} %get-tuple-element.94.refs_0_, f32[2048,128]{1,0:T(8,128)} %get-tuple-element.71.rec.refs_1_, f32[2048,768]{1,0:T(8,128)} %get-tuple-element.91.refs_2_, bf16[2048,512]{1,0:T(8,128)(2,1)} %get-tuple-element.92.refs_3_, ...), custom_call_target="tpu_custom_call" | custom-call | bytes 36900 | tf_op jit(solution)/shard_map/rear/pallas_call | solution.py:635
  230.1 10.3 %fusion.refs_1_.refs_2_.refs_3_.refs_4_ = f32[1024,1408]{1,0:T(8,128)S(1)} fusion(bf16[2048,1024]{1,0:T(8,128)(2,1)} %get-tuple-element.103, bf16[1024,1408]{1,0:T(8,128)(2,1)} %get-tuple-element.105, bf16[1024,1408]{1,0:T(8,128)(2,1)} %get-tuple-element.104), kind=kOutput, calls=%fused_computation | convolution fusion | flops 5917114368 | bytes 15728640 | tf_op jit(solution)/shard_map/dot_general | solution.py:1157
  240.4 2.5 copy-done
  244.8 5.8 %trade.3 = (bf16[1024,1024]{1,0:T(8,128)(2,1)}, bf16[1024,1024]{1,0:T(8,128)(2,1)}) custom-call(bf16[1024,1024]{1,0:T(8,128)(2,1)} %get-tuple-element.99.refs_8_.refs_0_, bf16[1024,1024]{1,0:T(8,128)(2,1)} %copy-done.11, bf16[1024,1024]{1,0:T(8,128)(2,1)} %get-tuple-element.102.refs_2_.refs_0_, f32[8,128]{1,0:T(8,128)} %broadcast_in_dim.54.refs_5_.refs_3_.refs_4_.refs_6_, ...), custom_call_target="tpu_custom_call" | custom-call | bytes 36900 | tf_op jit(solution)/shard_map/trade/pallas_call | solution.py:787
  250.6 6.0 %collective-permute-done.22.refs_1_.refs_2_ = bf16[1024,1024]{1,0:T(8,128)(2,1)S(1)} collective-permute-done((bf16[1024,1024]{1,0:T(8,128)(2,1)}, bf16[1024,1024]{1,0:T(8,128)(2,1)S(1)}, u32[]{:S(2)}, u32[]{:S(2)}) %collective-permute-start.22) | collective-permute-done | bytes 2097184 | tf_op jit(solution)/shard_map/ppermute | solution.py:824
  257.9 4.3 join.6.refs_6_.refs_0_
  262.2 2.0 collective-permute-start.23
  264.2 9.0 %collective-permute-start.21 = (bf16[1024,1024]{1,0:T(8,128)(2,1)}, bf16[1024,1024]{1,0:T(8,128)(2,1)S(1)}, u32[]{:S(2)}, u32[]{:S(2)}) collective-permute-start(bf16[1024,1024]{1,0:T(8,128)(2,1)} %get-tuple-element.106), channel_id=1, source_target_pairs={{0,1},{1,0},{2,3},{3,2},{4,5},{5,4},{6,7},{7,6},{8,9},{9,8},{10,11... | collective-permute-start | bytes 6291464 | tf_op jit(solution)/shard_map/ppermute | solution.py:824
  273.8 5.2 %settle.2.refs_2_.refs_3_.refs_5_ = bf16[2048,1024]{1,0:T(8,128)(2,1)} custom-call(bf16[2048,1024]{1,0:T(8,128)(2,1)} %bitcast.70, f32[8,2048]{1,0:T(8,128)} %get-tuple-element.79.sums.refs_1_, bf16[1024,1024]{1,0:T(8,128)(2,1)} %copy-done.4, bf16[1024,1024]{1,0:T(8,128)(2,1)} %get-tuple-element.101.refs_9_.refs_3_, ...), custom_call_target="tpu_custom_call" | custom-call | bytes 36900 | tf_op jit(solution)/shard_map/settle/pallas_call | solution.py:700
  279.0 4.8 %other_core.1 = bf16[512,1920]{1,0:T(8,128)(2,1)} custom-call(s32[3]{0:T(128)} %pad_add_fusion.2.refs_0_, f32[1024,1408]{1,0:T(8,128)} %copy-done, f32[1024,512]{1,0:T(8,128)} %convolution_bitcast_fusion.refs_11_.refs_2_.refs_5_.refs_6_, bf16[2048,1024]{1,0:T(8,128)(2,1)} %settle.2.refs_2_.refs_3_.refs_5_), custom_call_target="tpu_custom_call" | custom-call | bytes 36900 | tf_op jit(solution)/shard_map/other_core/pallas_call | solution.py:883
  283.8 4.3 join.7.refs_11_.refs_2_.refs_4_
  289.4 6.5 %split.1 = (f32[256,1024]{1,0:T(8,128)}, bf16[256,1024]{1,0:T(8,128)(2,1)}, f32[256,896]{1,0:T(8,128)}, bf16[256,896]{1,0:T(8,128)(2,1)}) custom-call(s32[3]{0:T(128)} %pad_add_fusion.2.refs_0_, f32[1024,1408]{1,0:T(8,128)} %copy-done, f32[1024,1408]{1,0:T(8,128)} %copy-done, f32[1024,1408]{1,0:T(8,128)} %copy-done, f32[1024,1408]{1,0:T(8,128)} %copy-done, ...), custom_call_target="tpu_custom_call" | custom-call | bytes 36900 | tf_op jit(solution)/shard_map/split/pallas_call | solution.py:883
  296.0 18.4 %collective-permute-done.21.refs_1_.refs_2_ = bf16[1024,1024]{1,0:T(8,128)(2,1)S(1)} collective-permute-done((bf16[1024,1024]{1,0:T(8,128)(2,1)}, bf16[1024,1024]{1,0:T(8,128)(2,1)S(1)}, u32[]{:S(2)}, u32[]{:S(2)}) %collective-permute-start.21) | collective-permute-done | bytes 2097184 | tf_op jit(solution)/shard_map/ppermute | solution.py:824
  315.7 4.5 join.8.refs_6_.refs_0_
  320.2 2.0 collective-permute-start.25
  329.5 5.3 %collective-permute-done.33 = f32[5120]{0:T(1024)S(1)} collective-permute-done((f32[5120]{0:T(1024)S(1)}, f32[5120]{0:T(1024)S(1)}, u32[]{:S(2)}, u32[]{:S(2)}) %collective-permute-start.33) | collective-permute-done | bytes 20512 | tf_op jit(solution)/shard_map/ppermute | solution.py:737
  335.9 5.3 %settle.3.refs_9_ = bf16[2048,1024]{1,0:T(8,128)(2,1)} custom-call(bf16[2048,1024]{1,0:T(8,128)(2,1)} %bitcast.71, f32[8,2048]{1,0:T(8,128)} %get-tuple-element.79.sums.refs_1_, bf16[1024,1024]{1,0:T(8,128)(2,1)} %copy-done.6, bf16[1024,1024]{1,0:T(8,128)(2,1)} %get-tuple-element.107.refs_2_.refs_3_, ...), custom_call_target="tpu_custom_call", output_to_operand_aliasing={{}: (5, {})} | custom-call | bytes 36900 | tf_op jit(solution)/shard_map/settle/pallas_call | solution.py:700
  342.1 3.6 second.1
  349.6 4.3 join.9.refs_7_.refs_4_
  355.2 22.7 %collective-permute-done.29.refs_3_ = bf16[1024,1024]{1,0:T(8,128)(2,1)} collective-permute-done((bf16[1024,1024]{1,0:T(8,128)(2,1)S(1)}, bf16[1024,1024]{1,0:T(8,128)(2,1)}, u32[]{:S(2)}, u32[]{:S(2)}) %collective-permute-start.29) | collective-permute-done | bytes 2097184 | tf_op jit(solution)/shard_map/ppermute | solution.py:816
  377.8 6.6 %finish.2 = (f32[2048,1024]{1,0:T(8,128)}, f32[128,1024]{1,0:T(8,128)}, f32[128,896]{1,0:T(8,128)}) custom-call(bf16[2048,1024]{1,0:T(8,128)(2,1)} %bitcast.72, bf16[2048,1024]{1,0:T(8,128)(2,1)} %bitcast.76, f32[8,1024]{1,0:T(8,128)} %get-tuple-element.110.refs_2_, ...), custom_call_target="tpu_custom_call", output_to_operand_aliasing={{1}: (8, {}), {2}: (9, {})} | custom-call | bytes 36900 | tf_op jit(solution)/shard_map/finish/pallas_call | solution.py:700
  386.9 7.7 %collective-permute-start.35 = (f32[34176]{0:T(1024)S(1)}, f32[34176]{0:T(1024)S(1)}, u32[]{:S(2)}, u32[]{:S(2)}) collective-permute-start(f32[34176]{0:T(1024)S(1)} %pad_maximum_fusion.1), channel_id=1, source_target_pairs={{0,1},{1,0},{2,3},{3,2},{4,5},{5,4},{6,7},{7,6},{8,9},{9,8},{10,11... | collective-permute-start | bytes 410120 | tf_op jit(solution)/shard_map/ppermute | solution.py:737
  396.4 31.8 %collective-permute-done.35 = f32[34176]{0:T(1024)S(1)} collective-permute-done((f32[34176]{0:T(1024)S(1)}, f32[34176]{0:T(1024)S(1)}, u32[]{:S(2)}, u32[]{:S(2)}) %collective-permute-start.35) | collective-permute-done | bytes 136736 | tf_op jit(solution)/shard_map/ppermute | solution.py:737
  429.8 4.9 %collective-permute-done.36 = f32[34176]{0:T(1024)S(1)} collective-permute-done((f32[34176]{0:T(1024)S(1)}, f32[34176]{0:T(1024)S(1)}, u32[]{:S(2)}, u32[]{:S(2)}) %collective-permute-start.36) | collective-permute-done | bytes 136736 | tf_op jit(solution)/shard_map/ppermute | solution.py:737
  437.1 6.6 %finish.3 = f32[2048,1024]{1,0:T(8,128)} custom-call(bf16[2048,1024]{1,0:T(8,128)(2,1)} %bitcast.73, bf16[2048,1024]{1,0:T(8,128)(2,1)} %bitcast.77, f32[8,1024]{1,0:T(8,128)} %get-tuple-element.110.refs_2_, bf16[1024,1024]{1,0:T(8,128)(2,1)} %collective-permute-done.28.refs_3_, ...), custom_call_target="tpu_custom_call", output_to_operand_aliasing={{}: (6, {})} | custom-call | bytes 36900 | tf_op jit(solution)/shard_map/finish/pallas_call | solution.py:700
  (218 shorter events, 64.9 us)
Async XLA Ops:
  7.2 27.3 %copy-start.20 = (s32[1,2048]{1,0:T(1,128)S(1)}, s32[1,2048]{1,0:T(1,128)}, u32[]{:S(2)}) copy-start(s32[1,2048]{1,0:T(1,128)} %param.17) | copy-start | bytes 24580
  7.2 25.8 %copy-start.36 = (f32[2,128]{1,0:T(2,128)S(1)}, f32[2,128]{1,0:T(2,128)}, u32[]{:S(2)}) copy-start(f32[2,128]{1,0:T(2,128)} %param.26) | copy-start | bytes 3076
  7.2 25.8 %copy-start.34 = (f32[512]{0:T(512)S(1)}, f32[512]{0:T(512)}, u32[]{:S(2)}) copy-start(f32[512]{0:T(512)} %param.24) | copy-start | bytes 6148
  7.2 25.8 %copy-start.33 = (f32[4,2,128]{2,1,0:T(2,128)S(1)}, f32[4,2,128]{2,1,0:T(2,128)}, u32[]{:S(2)}) copy-start(f32[4,2,128]{2,1,0:T(2,128)} %param.25) | copy-start | bytes 12292
  7.2 26.6 %copy-start.32 = (f32[4,512]{1,0:T(4,128)S(1)}, f32[4,512]{1,0:T(4,128)}, u32[]{:S(2)}) copy-start(f32[4,512]{1,0:T(4,128)} %param.23) | copy-start | bytes 24580
  7.2 61.7 %all-gather.2.cloned.1.call-start = ((), (), s32[]{:S(2)}) async-start(), calls=%async_computation | async-start | bytes 1179648 | tf_op jit(solution)/shard_map/all_gather | solution.py:1047
  10.9 28.2 %copy-start.7 = (bf16[128,1408]{1,0:T(8,128)(2,1)}, bf16[128,1408]{1,0:T(8,128)(2,1)S(1)}, u32[]{:S(2)}) copy-start(bf16[128,1408]{1,0:T(8,128)(2,1)S(1)} %concatenate.56.refs_0_) | copy-start | bytes 1081348
  10.9 13.2 %collective-permute-start.2 = (bf16[128,1408]{1,0:T(8,128)(2,1)S(1)}, bf16[128,1408]{1,0:T(8,128)(2,1)S(1)}, u32[]{:S(2)}, u32[]{:S(2)}) collective-permute-start(bf16[128,1408]{1,0:T(8,128)(2,1)S(1)} %concatenate.56.refs_0_), channel_id=1, source_target_pairs={{0,8},{8,0},{16,24},{24,16},{1,9},{9,1},{17,25},{25,17},{2,10},{10... | collective-permute-start | bytes 1081352 | tf_op jit(solution)/shard_map/ppermute | solution.py:988
  13.9 10.7 %collective-permute-start.3 = (bf16[128,1408]{1,0:T(8,128)(2,1)S(1)}, bf16[128,1408]{1,0:T(8,128)(2,1)S(1)}, u32[]{:S(2)}, u32[]{:S(2)}) collective-permute-start(bf16[128,1408]{1,0:T(8,128)(2,1)S(1)} %concatenate.56.refs_0_), channel_id=1, source_target_pairs={{0,16},{8,24},{16,0},{24,8},{1,17},{9,25},{17,1},{25,9},{2,18},{10... | collective-permute-start | bytes 1081352 | tf_op jit(solution)/shard_map/ppermute | solution.py:988
  15.4 23.6 %collective-permute-start.6 = (bf16[128,1408]{1,0:T(8,128)(2,1)S(1)}, bf16[128,1408]{1,0:T(8,128)(2,1)S(1)}, u32[]{:S(2)}, u32[]{:S(2)}) collective-permute-start(bf16[128,1408]{1,0:T(8,128)(2,1)S(1)} %concatenate.56.refs_0_), channel_id=1, source_target_pairs={{0,4},{4,0},{1,5},{5,1},{2,6},{6,2},{3,7},{7,3},{8,12},{12,8},{9,1... | collective-permute-start | bytes 1081352 | tf_op jit(solution)/shard_map/ppermute | solution.py:988
  16.1 18.4 %collective-permute-start.1 = (s32[3]{0:T(128)S(1)}, s32[3]{0:T(128)S(1)}, u32[]{:S(2)}, u32[]{:S(2)}) collective-permute-start(s32[3]{0:T(128)S(1)} %slice_bitcast_fusion.5), channel_id=1, source_target_pairs={{0,4},{1,5},{2,6},{3,7},{8,12},{9,13},{10,14},{11,15},{16,20},{17,... | collective-permute-start | bytes 44 | tf_op jit(solution)/shard_map/ppermute | solution.py:722
  19.3 17.4 %collective-permute-start = (bf16[16,1024]{1,0:T(8,128)(2,1)S(1)}, bf16[16,1024]{1,0:T(8,128)(2,1)S(1)}, u32[]{:S(2)}, u32[]{:S(2)}) collective-permute-start(bf16[16,1024]{1,0:T(8,128)(2,1)S(1)} %slice_bitcast_fusion.2), channel_id=1, source_target_pairs={{0,4},{1,5},{2,6},{3,7},{8,12},{9,13},{10,14},{11,15},{16,20},{17,... | collective-permute-start | bytes 98312 | tf_op jit(solution)/shard_map/ppermute | solution.py:722
  24.0 5.9 %collective-permute-start.5 = (bf16[64,1408]{1,0:T(8,128)(2,1)S(1)}, bf16[64,1408]{1,0:T(8,128)(2,1)S(1)}, u32[]{:S(2)}, u32[]{:S(2)}) collective-permute-start(bf16[64,1408]{1,0:T(8,128)(2,1)S(1)} %slice.204), channel_id=1, source_target_pairs={{0,16},{8,24},{16,0},{24,8},{1,17},{9,25},{17,1},{25,9},{2,18},{10... | collective-permute-start | bytes 540680 | tf_op jit(solution)/shard_map/ppermute | solution.py:988
  24.6 5.6 %collective-permute-start.4 = (bf16[64,1408]{1,0:T(8,128)(2,1)S(1)}, bf16[64,1408]{1,0:T(8,128)(2,1)S(1)}, u32[]{:S(2)}, u32[]{:S(2)}) collective-permute-start(bf16[64,1408]{1,0:T(8,128)(2,1)S(1)} %slice.203), channel_id=1, source_target_pairs={{0,8},{8,0},{16,24},{24,16},{1,9},{9,1},{17,25},{25,17},{2,10},{10... | collective-permute-start | bytes 540680 | tf_op jit(solution)/shard_map/ppermute | solution.py:988
  35.8 3.2 collective-permute-start.7
  35.8 3.2 collective-permute-start.8
  36.5 2.4 collective-permute-start.10
  36.7 2.3 collective-permute-start.9
  39.9 27.7 %copy-start.38 = (f32[8]{0:T(128)S(1)}, f32[8]{0:T(128)}, u32[]{:S(2)}) copy-start(f32[8]{0:T(128)} %param.29) | copy-start | bytes 100
  39.9 27.8 %copy-start.35 = (f32[512]{0:T(512)S(1)}, f32[512]{0:T(512)}, u32[]{:S(2)}) copy-start(f32[512]{0:T(512)} %param.30) | copy-start | bytes 6148
  65.5 3.4 collective-permute-start.11
  88.1 4.6 %collective-permute-start.12 = (f32[8,2048]{1,0:T(8,128)}, f32[8,2048]{1,0:T(8,128)S(1)}, u32[]{:S(2)}, u32[]{:S(2)}) collective-permute-start(f32[8,2048]{1,0:T(8,128)} %get-tuple-element.76.own), channel_id=1, source_target_pairs={{0,1},{1,0},{2,3},{3,2},{4,5},{5,4},{6,7},{7,6},{8,9},{9,8},{10,11... | collective-permute-start | bytes 196616 | tf_op jit(solution)/shard_map/ppermute | solution.py:842
  89.7 7.9 %collective-permute-start.13 = (f32[8,2048]{1,0:T(8,128)}, f32[8,2048]{1,0:T(8,128)S(1)}, u32[]{:S(2)}, u32[]{:S(2)}) collective-permute-start(f32[8,2048]{1,0:T(8,128)} %get-tuple-element.76.own), channel_id=1, source_target_pairs={{0,2},{1,3},{2,0},{3,1},{4,6},{5,7},{6,4},{7,5},{8,10},{9,11},{10,... | collective-permute-start | bytes 196616 | tf_op jit(solution)/shard_map/ppermute | solution.py:842
  92.3 6.3 %collective-permute-start.14 = (f32[8,2048]{1,0:T(8,128)}, f32[8,2048]{1,0:T(8,128)S(1)}, u32[]{:S(2)}, u32[]{:S(2)}) collective-permute-start(f32[8,2048]{1,0:T(8,128)} %get-tuple-element.76.own), channel_id=1, source_target_pairs={{0,3},{1,2},{2,1},{3,0},{4,7},{5,6},{6,5},{7,4},{8,11},{9,10},{10,... | collective-permute-start | bytes 196616 | tf_op jit(solution)/shard_map/ppermute | solution.py:842
  100.8 49.5 %collective-permute-start.16 = (bf16[1024,1024]{1,0:T(8,128)(2,1)}, bf16[1024,1024]{1,0:T(8,128)(2,1)}, u32[]{:S(2)}, u32[]{:S(2)}) collective-permute-start(bf16[1024,1024]{1,0:T(8,128)(2,1)} %get-tuple-element.81.refs_0_), channel_id=1, source_target_pairs={{0,1},{3,2},{4,5},{7,6},{8,9},{11,10},{12,13},{15,14},{16,17},{19,... | collective-permute-start | bytes 6291464 | tf_op jit(solution)/shard_map/ppermute | solution.py:804
  105.2 15.6 %copy-start.1 = (bf16[1,2048,1024]{2,1,0:T(8,128)(2,1)S(1)}, bf16[1,2048,1024]{2,1,0:T(8,128)(2,1)}, u32[]{:S(2)}) copy-start(bf16[1,2048,1024]{2,1,0:T(8,128)(2,1)} %param.18) | copy-start | bytes 12582916
  119.5 9.3 %collective-permute-start.17 = (f32[128,512]{1,0:T(8,128)}, f32[128,512]{1,0:T(8,128)S(1)}, u32[]{:S(2)}, u32[]{:S(2)}) collective-permute-start(f32[128,512]{1,0:T(8,128)} %get-tuple-element.87), channel_id=1, source_target_pairs={{4,0},{5,1},{6,2},{7,3},{12,8},{13,9},{14,10},{15,11},{20,16},{21,... | collective-permute-start | bytes 786440 | tf_op jit(solution)/shard_map/ppermute | solution.py:722
  126.2 67.4 %collective-permute-start.15 = (bf16[1024,1024]{1,0:T(8,128)(2,1)S(1)}, bf16[1024,1024]{1,0:T(8,128)(2,1)}, u32[]{:S(2)}, u32[]{:S(2)}) collective-permute-start(bf16[1024,1024]{1,0:T(8,128)(2,1)S(1)} %copy-done.5), channel_id=1, source_target_pairs={{0,1},{3,2},{4,5},{7,6},{8,9},{11,10},{12,13},{15,14},{16,17},{19,... | collective-permute-start | bytes 6291464 | tf_op jit(solution)/shard_map/ppermute | solution.py:804
  154.7 39.0 %collective-permute-start.18 = (bf16[1024,1024]{1,0:T(8,128)(2,1)}, bf16[1024,1024]{1,0:T(8,128)(2,1)}, u32[]{:S(2)}, u32[]{:S(2)}) collective-permute-start(bf16[1024,1024]{1,0:T(8,128)(2,1)} %join.5.refs_11_.refs_2_), channel_id=1, source_target_pairs={{1,2},{2,1},{5,6},{6,5},{9,10},{10,9},{13,14},{14,13},{17,18},{18,... | collective-permute-start | bytes 6291464 | tf_op jit(solution)/shard_map/ppermute | solution.py:813
  201.7 41.7 %collective-permute-start.19 = (bf16[1024,1024]{1,0:T(8,128)(2,1)}, bf16[1024,1024]{1,0:T(8,128)(2,1)S(1)}, u32[]{:S(2)}, u32[]{:S(2)}) collective-permute-start(bf16[1024,1024]{1,0:T(8,128)(2,1)} %get-tuple-element.99.refs_8_.refs_0_), channel_id=1, source_target_pairs={{1,2},{2,1},{5,6},{6,5},{9,10},{10,9},{13,14},{14,13},{17,18},{18,... | collective-permute-start | bytes 6291464 | tf_op jit(solution)/shard_map/ppermute | solution.py:813
  202.5 54.0 %collective-permute-start.22 = (bf16[1024,1024]{1,0:T(8,128)(2,1)}, bf16[1024,1024]{1,0:T(8,128)(2,1)S(1)}, u32[]{:S(2)}, u32[]{:S(2)}) collective-permute-start(bf16[1024,1024]{1,0:T(8,128)(2,1)} %get-tuple-element.108), channel_id=1, source_target_pairs={{0,1},{1,0},{2,3},{3,2},{4,5},{5,4},{6,7},{7,6},{8,9},{9,8},{10,11... | collective-permute-start | bytes 6291464 | tf_op jit(solution)/shard_map/ppermute | solution.py:824
  215.2 3.1 collective-permute-start.20
  262.2 21.6 %collective-permute-start.23 = (bf16[1024,1024]{1,0:T(8,128)(2,1)}, bf16[1024,1024]{1,0:T(8,128)(2,1)}, u32[]{:S(2)}, u32[]{:S(2)}) collective-permute-start(bf16[1024,1024]{1,0:T(8,128)(2,1)} %join.6.refs_6_.refs_0_), channel_id=1, source_target_pairs={{1,2},{2,1},{5,6},{6,5},{9,10},{10,9},{13,14},{14,13},{17,18},{18,... | collective-permute-start | bytes 6291464 | tf_op jit(solution)/shard_map/ppermute | solution.py:813
  264.2 50.1 %collective-permute-start.21 = (bf16[1024,1024]{1,0:T(8,128)(2,1)}, bf16[1024,1024]{1,0:T(8,128)(2,1)S(1)}, u32[]{:S(2)}, u32[]{:S(2)}) collective-permute-start(bf16[1024,1024]{1,0:T(8,128)(2,1)} %get-tuple-element.106), channel_id=1, source_target_pairs={{0,1},{1,0},{2,3},{3,2},{4,5},{5,4},{6,7},{7,6},{8,9},{9,8},{10,11... | collective-permute-start | bytes 6291464 | tf_op jit(solution)/shard_map/ppermute | solution.py:824
  283.8 4.3 collective-permute-start.24
  320.2 29.4 %collective-permute-start.25 = (bf16[1024,1024]{1,0:T(8,128)(2,1)}, bf16[1024,1024]{1,0:T(8,128)(2,1)}, u32[]{:S(2)}, u32[]{:S(2)}) collective-permute-start(bf16[1024,1024]{1,0:T(8,128)(2,1)} %join.8.refs_6_.refs_0_), channel_id=1, source_target_pairs={{1,2},{2,1},{5,6},{6,5},{9,10},{10,9},{13,14},{14,13},{17,18},{18,... | collective-permute-start | bytes 6291464 | tf_op jit(solution)/shard_map/ppermute | solution.py:813
  322.2 55.7 %collective-permute-start.29 = (bf16[1024,1024]{1,0:T(8,128)(2,1)S(1)}, bf16[1024,1024]{1,0:T(8,128)(2,1)}, u32[]{:S(2)}, u32[]{:S(2)}) collective-permute-start(bf16[1024,1024]{1,0:T(8,128)(2,1)S(1)} %copy-done.2), channel_id=1, source_target_pairs={{1,0},{2,3},{5,4},{6,7},{9,8},{10,11},{13,12},{14,15},{17,16},{18,... | collective-permute-start | bytes 6291464 | tf_op jit(solution)/shard_map/ppermute | solution.py:816
  324.9 16.2 %collective-permute-start.26 = (bf16[256,1024]{1,0:T(8,128)(2,1)}, bf16[256,1024]{1,0:T(8,128)(2,1)S(1)}, u32[]{:S(2)}, u32[]{:S(2)}) collective-permute-start(bf16[256,1024]{1,0:T(8,128)(2,1)} %get-tuple-element.109.refs_3_), channel_id=1, source_target_pairs={{0,8},{8,0},{16,24},{24,16},{1,9},{9,1},{17,25},{25,17},{2,10},{10... | collective-permute-start | bytes 1572872 | tf_op jit(solution)/shard_map/ppermute | solution.py:918
  325.4 15.7 %collective-permute-start.27 = (bf16[256,896]{1,0:T(8,128)(2,1)}, bf16[256,896]{1,0:T(8,128)(2,1)S(1)}, u32[]{:S(2)}, u32[]{:S(2)}) collective-permute-start(bf16[256,896]{1,0:T(8,128)(2,1)} %get-tuple-element.113), channel_id=1, source_target_pairs={{0,16},{8,24},{16,0},{24,8},{1,17},{9,25},{17,1},{25,9},{2,18},{10... | collective-permute-start | bytes 1376264 | tf_op jit(solution)/shard_map/ppermute | solution.py:918
  326.8 1.3 collective-permute-start.32
  328.0 6.8 %collective-permute-start.33 = (f32[5120]{0:T(1024)S(1)}, f32[5120]{0:T(1024)S(1)}, u32[]{:S(2)}, u32[]{:S(2)}) collective-permute-start(f32[5120]{0:T(1024)S(1)} %fusion.22), channel_id=1, source_target_pairs={{0,8},{8,0},{16,24},{24,16},{1,9},{9,1},{17,25},{25,17},{2,10},{10... | collective-permute-start | bytes 61448 | tf_op jit(solution)/shard_map/ppermute | solution.py:737
  334.8 11.5 %collective-permute-start.34 = (f32[5120]{0:T(1024)S(1)}, f32[5120]{0:T(1024)S(1)}, u32[]{:S(2)}, u32[]{:S(2)}) collective-permute-start(f32[5120]{0:T(1024)S(1)} %add.90), channel_id=1, source_target_pairs={{0,16},{8,24},{16,0},{24,8},{1,17},{9,25},{17,1},{25,9},{2,18},{10... | collective-permute-start | bytes 61448 | tf_op jit(solution)/shard_map/ppermute | solution.py:737
  345.7 38.7 %collective-permute-start.30 = (bf16[128,896]{1,0:T(8,128)(2,1)}, bf16[128,896]{1,0:T(8,128)(2,1)S(1)}, u32[]{:S(2)}, u32[]{:S(2)}) collective-permute-start(bf16[128,896]{1,0:T(8,128)(2,1)} %get-tuple-element.119), channel_id=1, source_target_pairs={{0,8},{8,0},{16,24},{24,16},{1,9},{9,1},{17,25},{25,17},{2,10},{10... | collective-permute-start | bytes 688136 | tf_op jit(solution)/shard_map/ppermute | solution.py:918
  348.8 36.7 %collective-permute-start.31 = (bf16[128,1024]{1,0:T(8,128)(2,1)}, bf16[128,1024]{1,0:T(8,128)(2,1)S(1)}, u32[]{:S(2)}, u32[]{:S(2)}) collective-permute-start(bf16[128,1024]{1,0:T(8,128)(2,1)} %get-tuple-element.114.refs_2_), channel_id=1, source_target_pairs={{0,16},{8,24},{16,0},{24,8},{1,17},{9,25},{17,1},{25,9},{2,18},{10... | collective-permute-start | bytes 786440 | tf_op jit(solution)/shard_map/ppermute | solution.py:918
  353.9 83.2 %collective-permute-start.28 = (bf16[1024,1024]{1,0:T(8,128)(2,1)}, bf16[1024,1024]{1,0:T(8,128)(2,1)}, u32[]{:S(2)}, u32[]{:S(2)}) collective-permute-start(bf16[1024,1024]{1,0:T(8,128)(2,1)} %join.9.refs_7_.refs_4_), channel_id=1, source_target_pairs={{1,0},{2,3},{5,4},{6,7},{9,8},{10,11},{13,12},{14,15},{17,16},{18,... | collective-permute-start | bytes 6291464 | tf_op jit(solution)/shard_map/ppermute | solution.py:816
  386.6 49.9 %copy-start.37 = (bf16[128]{0:T(256)(128)(2,1)S(1)}, bf16[128]{0:T(256)(128)(2,1)}, u32[]{:S(2)}) copy-start(bf16[128]{0:T(256)(128)(2,1)} %param.19) | copy-start | bytes 772
  386.9 41.3 %collective-permute-start.35 = (f32[34176]{0:T(1024)S(1)}, f32[34176]{0:T(1024)S(1)}, u32[]{:S(2)}, u32[]{:S(2)}) collective-permute-start(f32[34176]{0:T(1024)S(1)} %pad_maximum_fusion.1), channel_id=1, source_target_pairs={{0,1},{1,0},{2,3},{3,2},{4,5},{5,4},{6,7},{7,6},{8,9},{9,8},{10,11... | collective-permute-start | bytes 410120 | tf_op jit(solution)/shard_map/ppermute | solution.py:737
  428.2 6.5 %collective-permute-start.36 = (f32[34176]{0:T(1024)S(1)}, f32[34176]{0:T(1024)S(1)}, u32[]{:S(2)}, u32[]{:S(2)}) collective-permute-start(f32[34176]{0:T(1024)S(1)} %fusion.21), channel_id=1, source_target_pairs={{0,2},{1,3},{2,0},{3,1},{4,6},{5,7},{6,4},{7,5},{8,10},{9,11},{10,... | collective-permute-start | bytes 410120 | tf_op jit(solution)/shard_map/ppermute | solution.py:737
  (29 other events, 108.8 us)
Sparse Core Ops, SparseCore 0:
  33.1 23.4 all-gather.1
